TPU v7x, 512 devices: a whole 4x4x16 slice. The times are simulated.
512 devices in a mesh: seq: 128 (over z_lo, x, y, core), chan: 4 (over z_hi).
Axes of the slice: x: 4, y: 4, z: 16 (z_hi: 4, z_lo: 4; z = z_hi * 4 + z_lo), core: 2. Of those that a mesh axis runs over, the one named last changes fastest.
Arguments:
- inputs: bfloat16 [16384, 4096], P('seq'), may hold values from -24 to 24
- proj_weight: bfloat16 [3, 256, 4096], P(None, 'chan'), may hold values from -0.09375 to 0.09375
- filters: float32 [16384, 256], P('seq', 'chan'), may hold values from -2 to 2
- out_grad: bfloat16 [16384, 256], P('seq', 'chan'), may hold values from -6 to 6
Outputs:
- gated: bfloat16 [16384, 256], P('seq', 'chan')
- weight_grad: bfloat16 [4096, 3, 256], P('seq', None, 'chan')
- input_grad: bfloat16 [16384, 4096], P('seq', 'chan')
All inputs are finite; a program needn't handle non-finite values.
Results may differ from a plain program's by a relative error of at most 0.023.
Values may be sent and summed in bfloat16 or wider, within the bound.
No kernel may reach another device: no remote copies, remote signals or barrier semaphores. Data moves between devices by JAX's collectives and lax.ppermute only.
A program may use at most 64 MiB of HBM per device.

v0:
```python
import math

import jax
import jax.numpy as jnp
from jax import lax
from jax.sharding import PartitionSpec as P


def square_table(size, sign):
    index_row = jnp.arange(size, dtype=jnp.int32)
    product = index_row[:, None] * index_row[None, :] % size
    angles = sign * 2.0 * math.pi / size * product.astype(jnp.float32)
    return (jnp.cos(angles), jnp.sin(angles))


def exact_dot(left, right):
    return jnp.dot(left, right, precision=lax.Precision.HIGHEST, preferred_element_type=jnp.float32)


def complex_dot(left_re, left_im, right_re, right_im):
    real_out = exact_dot(left_re, right_re) - exact_dot(left_im, right_im)
    imag_out = exact_dot(left_re, right_im) + exact_dot(left_im, right_re)
    return (real_out, imag_out)


def spread(real_part, imag_part):
    got = lax.all_to_all(
        jnp.stack([real_part, imag_part])[:, None].astype(jnp.bfloat16),
        "seq",
        split_axis=2,
        concat_axis=1,
        tiled=True,
    ).astype(jnp.float32)
    return (got[0], got[1])


def collect(real_part, imag_part):
    got = lax.all_to_all(
        jnp.stack([real_part, imag_part]).astype(jnp.bfloat16),
        "seq",
        split_axis=1,
        concat_axis=2,
        tiled=True,
    ).astype(jnp.float32)
    return (got[0, 0], got[1, 0])


def rotate(real_part, imag_part, angles):
    cosine = jnp.cos(angles)
    sine = jnp.sin(angles)
    return (real_part * cosine - imag_part * sine, real_part * sine + imag_part * cosine)


def forward_transform(real_part, imag_part, position, parts, length):
    rows, cols = real_part.shape
    block = rows // parts
    spread_re, spread_im = spread(real_part, imag_part)
    table_re, table_im = square_table(parts, -1.0)
    mid_re, mid_im = complex_dot(
        table_re,
        table_im,
        spread_re.reshape(parts, block * cols),
        spread_im.reshape(parts, block * cols),
    )
    local_t = position * block + jnp.arange(block, dtype=jnp.int32)
    freq = jnp.arange(parts, dtype=jnp.int32)
    turns = freq[:, None] * local_t[None, :] % length
    angles = (-2.0 * math.pi / length * turns.astype(jnp.float32))[:, :, None]
    rot_re, rot_im = rotate(
        mid_re.reshape(parts, block, cols), mid_im.reshape(parts, block, cols), angles
    )
    back_re, back_im = collect(rot_re, rot_im)
    table_re, table_im = square_table(rows, -1.0)
    return complex_dot(table_re, table_im, back_re, back_im)


def inverse_transform(real_part, imag_part, position, parts, length):
    rows, cols = real_part.shape
    block = rows // parts
    table_re, table_im = square_table(rows, 1.0)
    first_re, first_im = complex_dot(table_re, table_im, real_part, imag_part)
    turns = jnp.arange(rows, dtype=jnp.int32) * position % length
    angles = (2.0 * math.pi / length * turns.astype(jnp.float32))[:, None]
    first_re, first_im = rotate(first_re, first_im, angles)
    spread_re, spread_im = spread(first_re, first_im)
    table_re, table_im = square_table(parts, 1.0)
    mid_re, mid_im = complex_dot(
        table_re,
        table_im,
        spread_re.reshape(parts, block * cols),
        spread_im.reshape(parts, block * cols),
    )
    back_re, back_im = collect(
        mid_re.reshape(parts, block, cols), mid_im.reshape(parts, block, cols)
    )
    inverse_scale = 1.0 / length
    return (back_re * inverse_scale, back_im * inverse_scale)


def arrange(real_part, imag_part):
    rows, cols = real_part.shape
    got = lax.all_to_all(
        jnp.stack([real_part, imag_part])[:, None].astype(jnp.bfloat16),
        "seq",
        split_axis=2,
        concat_axis=1,
        tiled=True,
    ).astype(jnp.float32)
    got = jnp.transpose(got, (0, 2, 1, 3)).reshape(2, rows, cols)
    return (got[0], got[1])


def disarrange(real_part, imag_part, parts):
    rows, cols = real_part.shape
    block = rows // parts
    stacked = jnp.stack([real_part, imag_part]).reshape(2, block, parts, cols)
    stacked = jnp.transpose(stacked, (0, 2, 1, 3))
    got = lax.all_to_all(
        stacked.astype(jnp.bfloat16), "seq", split_axis=1, concat_axis=2, tiled=True
    ).astype(stacked.dtype)
    return (got[0, 0], got[1, 0])


def shards(inputs, proj_weight, filters, out_grad):
    f32 = jnp.float32
    bf16 = jnp.bfloat16
    parts = lax.axis_size("seq")
    position = lax.axis_index("seq")
    rows, width = inputs.shape
    chans = filters.shape[1]
    length = rows * parts
    flat_w = proj_weight.reshape(3 * chans, width)
    fields = lax.dot_general(
        inputs, flat_w, (((1,), (1,)), ((), ())), preferred_element_type=f32
    ).astype(bf16)
    query = fields[:, :chans].astype(f32)
    keys = fields[:, chans : 2 * chans].astype(f32)
    values = fields[:, 2 * chans :].astype(f32)
    mixed = keys * values
    global_n = position * rows + jnp.arange(rows, dtype=jnp.int32)
    theta = (-math.pi / length * global_n.astype(f32))[:, None]
    cos_t = jnp.cos(theta)
    sin_t = jnp.sin(theta)
    zero_cols = jnp.zeros_like(mixed)
    in_re = jnp.concatenate([mixed, mixed * cos_t, filters, filters * cos_t], axis=1)
    in_im = jnp.concatenate([zero_cols, mixed * sin_t, zero_cols, filters * sin_t], axis=1)
    spec_re, spec_im = forward_transform(in_re, in_im, position, parts, length)
    spec_re, spec_im = arrange(spec_re, spec_im)
    sig_re = spec_re[:, : 2 * chans]
    sig_im = spec_im[:, : 2 * chans]
    filt_re = spec_re[:, 2 * chans :]
    filt_im = spec_im[:, 2 * chans :]
    prod_re = sig_re * filt_re - sig_im * filt_im
    prod_im = sig_re * filt_im + sig_im * filt_re
    prod_re, prod_im = disarrange(prod_re, prod_im, parts)
    out_re, out_im = inverse_transform(prod_re, prod_im, position, parts, length)
    conv = 0.5 * (out_re[:, :chans] + cos_t * out_re[:, chans:] + sin_t * out_im[:, chans:])
    gated = (query * conv).astype(bf16)
    grad = out_grad.astype(f32)
    grad_query = (grad * conv).astype(bf16)
    grad_conv = grad * query
    back_in_re = jnp.concatenate([grad_conv, grad_conv * cos_t], axis=1)
    back_in_im = jnp.concatenate([zero_cols, grad_conv * sin_t], axis=1)
    back_re, back_im = forward_transform(back_in_re, back_in_im, position, parts, length)
    back_re, back_im = arrange(back_re, back_im)
    corr_re = back_re * filt_re + back_im * filt_im
    corr_im = back_im * filt_re - back_re * filt_im
    corr_re, corr_im = disarrange(corr_re, corr_im, parts)
    res_re, res_im = inverse_transform(corr_re, corr_im, position, parts, length)
    grad_mixed = 0.5 * (res_re[:, :chans] + cos_t * res_re[:, chans:] + sin_t * res_im[:, chans:])
    grad_key = (grad_mixed * values).astype(bf16)
    grad_value = (grad_mixed * keys).astype(bf16)
    grads = jnp.concatenate([grad_query, grad_key, grad_value], axis=1)
    partial_sum = jnp.dot(grads, flat_w, preferred_element_type=f32)
    input_grad = (
        lax.psum_scatter(partial_sum.astype(jnp.bfloat16), "chan", scatter_dimension=1, tiled=True)
        .astype(jnp.float32)
        .astype(bf16)
    )
    share = width // parts
    summed = lax.psum_scatter(
        lax.dot_general(inputs, grads, (((0,), (0,)), ((), ())), preferred_element_type=f32),
        "seq",
        scatter_dimension=0,
        tiled=True,
    )
    scale = 1.0 / math.sqrt(length)
    weight_grad = (summed * scale).reshape(share, 3, chans).astype(bf16)
    return (gated, weight_grad, input_grad)


def solution(mesh):
    return jax.shard_map(
        shards,
        mesh=mesh,
        in_specs=(P("seq", None), P(None, "chan", None), P("seq", "chan"), P("seq", "chan")),
        out_specs=(P("seq", "chan"), P("seq", None, "chan"), P("seq", "chan")),
        check_vma=False,
    )
```

profile of v0, /device:TPU:1, one launch (start us, length us, event | category | flops | bytes accessed | tf_op | source)
XLA Modules:
  0.0 978.3 jit_solution(5970264782020930134)
XLA Ops:
  7.2 1.3 copy-done
  8.6 1.8 convolution_convert_fusion.1
  11.2 13.8 %all-to-all-start.6 = ((bf16[2,1,128,128]{3,0,1,2:T(2,128)(2,1)}), bf16[2,1,128,128]{3,0,1,2:T(2,128)(2,1)S(1)}, u32[]{:S(2)}, u32[]{:S(2)}) async-start(bf16[2,1,128,128]{3,0,1,2:T(2,128)(2,1)} %copy.82), calls=%async_computation.6 | async-start | bytes 131072 | tf_op jit(solution)/shard_map/all_to_all | solution.py:27
  26.0 9.1 all-to-all-done.6
  35.1 5.9 all-to-all-start
  43.5 8.6 all-to-all-done
  52.1 5.7 all-to-all-start.7
  60.6 7.4 all-to-all-done.7
  68.0 6.4 all-to-all-start.1
  76.8 8.6 all-to-all-done.1
  85.4 5.7 all-to-all-start.8
  93.9 7.4 all-to-all-done.8
  101.3 5.9 all-to-all-start.2
  107.2 11.0 %all-to-all-done.2 = bf16[2,1,128,256]{3,0,1,2:T(2,128)(2,1)S(1)} async-done(((bf16[2,1,128,256]{3,0,1,2:T(2,128)(2,1)}), bf16[2,1,128,256]{3,0,1,2:T(2,128)(2,1)S(1)}, u32[]{:S(2)}, u32[]{:S(2)}) %all-to-all-start.2) | async-done | bytes 131104 | tf_op jit(solution)/shard_map/all_to_all | solution.py:102
  119.2 5.7 all-to-all-start.9
  125.7 9.3 all-to-all-done.9
  135.0 6.1 all-to-all-start.3
  142.9 8.4 all-to-all-done.3
  153.7 5.9 all-to-all-start.10
  160.3 9.4 all-to-all-done.10
  169.7 5.9 all-to-all-start.4
  178.1 7.7 all-to-all-done.4
  185.8 6.2 all-to-all-start.11
  194.5 7.6 all-to-all-done.11
  202.0 5.9 all-to-all-start.5
  208.2 9.9 %all-to-all-done.5 = bf16[2,128,1,128]{3,0,2,1:T(2,128)(2,1)S(1)} async-done(((bf16[2,128,1,128]{3,0,2,1:T(2,128)(2,1)}), bf16[2,128,1,128]{3,0,2,1:T(2,128)(2,1)S(1)}, u32[]{:S(2)}, u32[]{:S(2)}) %all-to-all-start.5) | async-done | bytes 65568 | tf_op jit(solution)/shard_map/all_to_all | solution.py:38
  218.9 2.2 convolution_bitcast_fusion
  221.1 5.1 copy.99
  226.3 1.5 convolution_convert_fusion
  227.8 679.9 %reduce-scatter.7.cloned.1.call-done = f32[32,192]{1,0:T(8,128)} async-done(((f32[4096,192]{1,0:T(8,128)}), f32[32,192]{1,0:T(8,128)}) %reduce-scatter.7.cloned.1.call-update) | async-done | bytes 24592
  907.7 0.9 copy.100
  909.3 61.9 %reduce-scatter.5.cloned.1.call-done = bf16[128,1024]{1,0:T(8,128)(2,1)} async-done(((bf16[128,4096]{1,0:T(8,128)(2,1)}), bf16[128,1024]{1,0:T(8,128)(2,1)}) %reduce-scatter.5.cloned.1.call-update) | async-done | bytes 262160 | tf_op jit(solution)/shard_map/reduce_scatter | solution.py:176
  (100 shorter events, 25.4 us)
Async XLA Ops:
  7.2 1.4 copy-start
  7.2 3.2 copy-start.2
  8.6 16.5 %copy-start.3 = (f32[128,64]{0,1:T(8,128)S(1)}, f32[128,64]{0,1:T(8,128)}, u32[]{:S(2)}) copy-start(f32[128,64]{0,1:T(8,128)} %param.6) | copy-start | bytes 98308
  11.2 23.9 %all-to-all-start.6 = ((bf16[2,1,128,128]{3,0,1,2:T(2,128)(2,1)}), bf16[2,1,128,128]{3,0,1,2:T(2,128)(2,1)S(1)}, u32[]{:S(2)}, u32[]{:S(2)}) async-start(bf16[2,1,128,128]{3,0,1,2:T(2,128)(2,1)} %copy.82), calls=%async_computation.6 | async-start | bytes 131072 | tf_op jit(solution)/shard_map/all_to_all | solution.py:27
  35.1 17.0 %all-to-all-start = ((bf16[2,1,128,256]{3,0,1,2:T(2,128)(2,1)}), bf16[2,1,128,256]{3,0,1,2:T(2,128)(2,1)S(1)}, u32[]{:S(2)}, u32[]{:S(2)}) async-start(bf16[2,1,128,256]{3,0,1,2:T(2,128)(2,1)} %copy.66), calls=%async_computation | async-start | bytes 262144 | tf_op jit(solution)/shard_map/all_to_all | solution.py:27
  52.1 15.9 %all-to-all-start.7 = ((bf16[2,128,1,128]{3,0,2,1:T(2,128)(2,1)}), bf16[2,128,1,128]{3,0,2,1:T(2,128)(2,1)S(1)}, u32[]{:S(2)}, u32[]{:S(2)}) async-start(bf16[2,128,1,128]{3,0,2,1:T(2,128)(2,1)} %copy.85), calls=%async_computation.7 | async-start | bytes 131072 | tf_op jit(solution)/shard_map/all_to_all | solution.py:38
  68.0 17.4 %all-to-all-start.1 = ((bf16[2,128,1,256]{3,0,2,1:T(2,128)(2,1)}), bf16[2,128,1,256]{3,0,2,1:T(2,128)(2,1)S(1)}, u32[]{:S(2)}, u32[]{:S(2)}) async-start(bf16[2,128,1,256]{3,0,2,1:T(2,128)(2,1)} %copy.69), calls=%async_computation.1 | async-start | bytes 262144 | tf_op jit(solution)/shard_map/all_to_all | solution.py:38
  85.4 15.9 %all-to-all-start.8 = ((bf16[2,1,128,128]{3,0,1,2:T(2,128)(2,1)}), bf16[2,1,128,128]{3,0,1,2:T(2,128)(2,1)S(1)}, u32[]{:S(2)}, u32[]{:S(2)}) async-start(bf16[2,1,128,128]{3,0,1,2:T(2,128)(2,1)} %copy.88), calls=%async_computation.8 | async-start | bytes 131072 | tf_op jit(solution)/shard_map/all_to_all | solution.py:102
  101.3 17.0 %all-to-all-start.2 = ((bf16[2,1,128,256]{3,0,1,2:T(2,128)(2,1)}), bf16[2,1,128,256]{3,0,1,2:T(2,128)(2,1)S(1)}, u32[]{:S(2)}, u32[]{:S(2)}) async-start(bf16[2,1,128,256]{3,0,1,2:T(2,128)(2,1)} %copy.72), calls=%async_computation.2 | async-start | bytes 262144 | tf_op jit(solution)/shard_map/all_to_all | solution.py:102
  119.2 15.8 %all-to-all-start.9 = ((bf16[2,128,1,128]{3,0,2,1:T(2,128)(2,1)}), bf16[2,128,1,128]{3,0,2,1:T(2,128)(2,1)S(1)}, u32[]{:S(2)}, u32[]{:S(2)}) async-start(bf16[2,128,1,128]{3,0,2,1:T(2,128)(2,1)} %copy.90), calls=%async_computation.9 | async-start | bytes 131072 | tf_op jit(solution)/shard_map/all_to_all | solution.py:118
  135.0 16.2 %all-to-all-start.3 = ((bf16[2,128,1,128]{3,0,2,1:T(2,128)(2,1)}), bf16[2,128,1,128]{3,0,2,1:T(2,128)(2,1)S(1)}, u32[]{:S(2)}, u32[]{:S(2)}) async-start(bf16[2,128,1,128]{3,0,2,1:T(2,128)(2,1)} %copy.74), calls=%async_computation.3 | async-start | bytes 131072 | tf_op jit(solution)/shard_map/all_to_all | solution.py:118
  153.7 16.0 %all-to-all-start.10 = ((bf16[2,1,128,128]{3,0,1,2:T(2,128)(2,1)}), bf16[2,1,128,128]{3,0,1,2:T(2,128)(2,1)S(1)}, u32[]{:S(2)}, u32[]{:S(2)}) async-start(bf16[2,1,128,128]{3,0,1,2:T(2,128)(2,1)} %copy.93), calls=%async_computation.10 | async-start | bytes 131072 | tf_op jit(solution)/shard_map/all_to_all | solution.py:27
  169.7 16.1 %all-to-all-start.4 = ((bf16[2,1,128,128]{3,0,1,2:T(2,128)(2,1)}), bf16[2,1,128,128]{3,0,1,2:T(2,128)(2,1)S(1)}, u32[]{:S(2)}, u32[]{:S(2)}) async-start(bf16[2,1,128,128]{3,0,1,2:T(2,128)(2,1)} %copy.77), calls=%async_computation.4 | async-start | bytes 131072 | tf_op jit(solution)/shard_map/all_to_all | solution.py:27
  185.8 16.3 %all-to-all-start.11 = ((bf16[2,128,1,128]{3,0,2,1:T(2,128)(2,1)}), bf16[2,128,1,128]{3,0,2,1:T(2,128)(2,1)S(1)}, u32[]{:S(2)}, u32[]{:S(2)}) async-start(bf16[2,128,1,128]{3,0,2,1:T(2,128)(2,1)} %copy.96), calls=%async_computation.11 | async-start | bytes 131072 | tf_op jit(solution)/shard_map/all_to_all | solution.py:38
  192.1 26.8 %copy-start.1 = (bf16[128,4096]{1,0:T(8,128)(2,1)S(1)}, bf16[128,4096]{1,0:T(8,128)(2,1)}, u32[]{:S(2)}) copy-start(bf16[128,4096]{1,0:T(8,128)(2,1)} %param.4) | copy-start | bytes 3145732
  202.0 16.1 %all-to-all-start.5 = ((bf16[2,128,1,128]{3,0,2,1:T(2,128)(2,1)}), bf16[2,128,1,128]{3,0,2,1:T(2,128)(2,1)S(1)}, u32[]{:S(2)}, u32[]{:S(2)}) async-start(bf16[2,128,1,128]{3,0,2,1:T(2,128)(2,1)} %copy.80), calls=%async_computation.5 | async-start | bytes 131072 | tf_op jit(solution)/shard_map/all_to_all | solution.py:38
  208.0 699.8 %reduce-scatter.7.cloned.1.call-start = ((), (), s32[]{:S(2)}) async-start(), calls=%async_computation.15 | async-start | bytes 4227072
  226.3 745.0 %reduce-scatter.5.cloned.1.call-start = ((), (), s32[]{:S(2)}) async-start(), calls=%async_computation.14 | async-start | bytes 1310720 | tf_op jit(solution)/shard_map/reduce_scatter | solution.py:176
Sparse Core Ops, SparseCore 0:
  226.4 681.3 reduce-scatter.6
  911.4 59.7 reduce-scatter.4
where the time goes:
time: 989 us; the launch traced here: 978 us
  waiting for transfers between devices  846 us (86%)
  starting transfers between devices  79.2 us (8%)
  matrix products  18.8 us (2%)
  local copies, waits for them, and re-layouts  18.2 us (2%)
  between operations  15 us (2%)
    unnamed x3, waiting for transfers between devices  680 us
    reduce_scatter x1, waiting for transfers between devices, shards(): lax.psum_scatter(partial_sum.astype(jnp.bfloat16), 'chan', scatter_dimens...  61.9 us
    all_to_all x4, waiting for transfers between devices, spread(): lax.all_to_all(jnp.stack([real_part, imag_part])[:, None].astype(jnp.bflo...  34.7 us
    all_to_all x4, waiting for transfers between devices, collect(): lax.all_to_all(jnp.stack([real_part, imag_part]).astype(jnp.bfloat16), 's...  33.4 us
    all_to_all x4, starting transfers between devices, spread(): lax.all_to_all(jnp.stack([real_part, imag_part])[:, None].astype(jnp.bflo...  31.5 us
    all_to_all x4, starting transfers between devices, collect(): lax.all_to_all(jnp.stack([real_part, imag_part]).astype(jnp.bfloat16), 's...  24.2 us
  transfers between devices with their start and end apart: 14, of which 14 were waited for; matrix products, arithmetic and copies ran while one was open for 2% of the time, Pallas kernels for 0%

commit v1 on v0

v1 whole, which is shorter than its diff:
```python
import math

import jax
import jax.numpy as jnp
import numpy as np
from jax import lax
from jax.experimental import pallas as pl
from jax.experimental.pallas import tpu as pltpu
from jax.sharding import Mesh, PartitionSpec as P

F32 = jnp.float32
BF16 = jnp.bfloat16
SEQ = ("z", "x", "y", "core")
ROWS = 128
CH = 64
VMEM_LIMIT = 48 * 1024 * 1024


def params(*semantics):
    return pltpu.CompilerParams(
        vmem_limit_bytes=VMEM_LIMIT, dimension_semantics=semantics or None
    )


def nt_dot(left, right):
    return lax.dot_general(left, right, (((1,), (1,)), ((), ())), preferred_element_type=F32)


def tn_dot(left, right):
    return lax.dot_general(left, right, (((0,), (0,)), ((), ())), preferred_element_type=F32)


def nn_dot(left, right):
    return jnp.dot(left, right, preferred_element_type=F32)


def tables():
    length = ROWS * ROWS
    index = np.arange(ROWS)
    first = np.exp(-2j * np.pi * np.outer(index + 0.25, index) / ROWS)
    twist = np.exp(-2j * np.pi * np.outer(index + 0.25, index) / length)
    second = np.exp(-2j * np.pi * np.outer(index, index) / ROWS)
    first_rows = np.concatenate([first.real, first.imag], axis=0)
    second_fwd = np.block([[second.real, second.imag], [-second.imag, second.real]])
    second_bwd = np.block([[second.real, -second.imag], [second.imag, second.real]])
    first_bwd = np.concatenate([first.real.T, first.imag.T], axis=1) / length
    as_bf16 = lambda x: jnp.asarray(x, dtype=BF16)
    as_f32 = lambda x: jnp.asarray(x, dtype=F32)
    return (
        as_bf16(first_rows),
        as_f32(twist.real),
        as_f32(twist.imag),
        as_bf16(second_fwd),
        as_bf16(second_bwd),
        as_bf16(first_bwd),
    )


def fields_kernel(x_ref, w_ref, filt_ref, grad_ref, fields_ref, send_ref, acc, scratch):
    step = pl.program_id(0)

    @pl.when(step == 0)
    def _():
        acc[...] = jnp.zeros_like(acc)

    acc[...] += nt_dot(w_ref[...], x_ref[...])

    @pl.when(step == pl.num_programs(0) - 1)
    def _():
        fields = acc[...].astype(BF16)
        fields_ref[0 : 3 * CH, :] = fields
        grad_t = grad_ref[...].astype(F32).T
        fields_ref[3 * CH : 4 * CH, :] = grad_t.astype(BF16)
        query = fields[0:CH].astype(F32)
        key = fields[CH : 2 * CH].astype(F32)
        value = fields[2 * CH : 3 * CH].astype(F32)
        filt_t = filt_ref[...].T
        scratch[pl.ds(0, CH, stride=4), :] = key * value
        scratch[pl.ds(1, CH, stride=4), :] = filt_t
        scratch[pl.ds(2, CH, stride=4), :] = grad_t * query
        scratch[pl.ds(3, CH, stride=4), :] = filt_t
        send_ref[...] = scratch[...].astype(BF16)


def fields_call(inputs, flat_w, filters, out_grad):
    width = inputs.shape[1]
    tile = 1024
    return pl.pallas_call(
        fields_kernel,
        grid=(width // tile,),
        in_specs=[
            pl.BlockSpec((ROWS, tile), lambda i: (0, i)),
            pl.BlockSpec((3 * CH, tile), lambda i: (0, i)),
            pl.BlockSpec((ROWS, CH), lambda i: (0, 0)),
            pl.BlockSpec((ROWS, CH), lambda i: (0, 0)),
        ],
        out_specs=[
            pl.BlockSpec((4 * CH, ROWS), lambda i: (0, 0)),
            pl.BlockSpec((4 * CH, ROWS), lambda i: (0, 0)),
        ],
        out_shape=[
            jax.ShapeDtypeStruct((4 * CH, ROWS), BF16),
            jax.ShapeDtypeStruct((4 * CH, ROWS), BF16),
        ],
        scratch_shapes=[
            pltpu.VMEM((3 * CH, ROWS), F32),
            pltpu.VMEM((4 * CH, ROWS), F32),
        ],
        compiler_params=params("arbitrary"),
        name="fields",
    )(inputs, flat_w, filters, out_grad)


def flip_kernel(x_ref, out_ref):
    step = pl.program_id(0)
    for x_y in range(16):
        block = x_ref[:, 64 * x_y : 64 * (x_y + 1)].astype(F32).T.astype(BF16)
        for core in range(2):
            out_ref[core, x_y, :, :] = block[32 * core : 32 * (core + 1), :]


def flip_call(inputs):
    out = pl.pallas_call(
        flip_kernel,
        grid=(4,),
        in_specs=[pl.BlockSpec((ROWS, 1024), lambda i: (0, i))],
        out_specs=pl.BlockSpec((2, 16, 32, ROWS), lambda i: (0, 0, i, 0)),
        out_shape=jax.ShapeDtypeStruct((2, 16, 128, ROWS), BF16),
        compiler_params=params("arbitrary"),
        name="flip",
    )(inputs)
    return out.reshape(4096, ROWS)


def conv_kernel(got_ref, e1_ref, twr_ref, twi_ref, e2_ref, e2b_ref, e1b_ref, out_ref, scratch):
    sign = jnp.where(lax.axis_index("core") == 0, 1.0, -1.0).astype(F32)
    scratch[...] = got_ref[...].astype(F32)
    signal = scratch[pl.ds(0, ROWS, stride=2), :].astype(BF16)
    filt = scratch[pl.ds(1, ROWS, stride=2), :].astype(BF16)
    twr, twi = twr_ref[...], twi_ref[...]

    both = nn_dot(e1_ref[...], jnp.concatenate([signal, filt], axis=1))

    def twisted(part):
        re, im = part[0:ROWS], part[ROWS:]
        return jnp.concatenate([re * twr - im * twi, re * twi + im * twr], axis=1)

    mid = jnp.concatenate([twisted(both[:, 0:ROWS]), twisted(both[:, ROWS:])], axis=0)
    spec = nn_dot(mid.astype(BF16), e2_ref[...])
    sig_re, sig_im = spec[0:ROWS, 0:ROWS], spec[0:ROWS, ROWS:]
    fil_re, fil_im = spec[ROWS:, 0:ROWS], spec[ROWS:, ROWS:] * sign
    prod_re = sig_re * fil_re - sig_im * fil_im
    prod_im = sig_re * fil_im + sig_im * fil_re
    prod = jnp.concatenate([prod_re, prod_im], axis=1).astype(BF16)
    back = nn_dot(prod, e2b_ref[...])
    re, im = back[:, 0:ROWS], back[:, ROWS:]
    stack = jnp.concatenate([re * twr + im * twi, im * twr - re * twi], axis=0).astype(BF16)
    out_ref[...] = nn_dot(e1b_ref[...], stack)


def conv_call(got):
    return pl.pallas_call(
        conv_kernel,
        out_shape=jax.ShapeDtypeStruct((ROWS, ROWS), F32),
        scratch_shapes=[pltpu.VMEM((2 * ROWS, ROWS), F32)],
        compiler_params=params(),
        name="conv",
    )(got, *tables())


def grads_of(got_ref, fields_ref):
    conv = got_ref[pl.ds(0, CH, stride=2), :]
    grad_mixed = got_ref[pl.ds(1, CH, stride=2), :]
    fields = fields_ref[...].astype(F32)
    query, key = fields[0:CH], fields[CH : 2 * CH]
    value, grad = fields[2 * CH : 3 * CH], fields[3 * CH :]
    gated = query * conv
    return gated, jnp.concatenate([grad * conv, grad_mixed * value, grad_mixed * key], axis=0)


def parts_kernel(chan_ref, got_ref, fields_ref, w_ref, gated_ref, grads_ref, *out_refs):
    step = pl.program_id(0)

    @pl.when(step == 0)
    def _():
        gated, grads = grads_of(got_ref, fields_ref)
        gated_ref[...] = gated.T.astype(BF16)
        grads_ref[...] = grads.T.astype(BF16)

    part = nn_dot(grads_ref[...], w_ref[...]).astype(BF16)
    for slab, out_ref in enumerate(out_refs):

        @pl.when(step == slab)
        def _(out_ref=out_ref):
            out_ref[...] = part


def parts_call(got, fields, flat_w):
    chan = lax.axis_index("chan").reshape(1)
    slab = flat_w.shape[1] // 4
    whole = lambda shape: pl.BlockSpec(shape, lambda i, chan: (0, 0))
    return pl.pallas_call(
        parts_kernel,
        grid_spec=pltpu.PrefetchScalarGridSpec(
            num_scalar_prefetch=1,
            grid=(4,),
            in_specs=[
                whole((ROWS, ROWS)),
                whole((4 * CH, ROWS)),
                pl.BlockSpec((3 * CH, slab), lambda i, chan: (0, lax.rem(chan[0] + i + 1, 4))),
            ],
            out_specs=[whole((ROWS, CH)), whole((ROWS, 3 * CH))] + [whole((ROWS, slab))] * 4,
        ),
        out_shape=[
            jax.ShapeDtypeStruct((ROWS, CH), BF16),
            jax.ShapeDtypeStruct((ROWS, 3 * CH), BF16),
        ]
        + [jax.ShapeDtypeStruct((ROWS, slab), BF16)] * 4,
        compiler_params=params("arbitrary"),
        name="parts",
    )(chan, got, fields, flat_w)


def share_kernel(flip_ref, grads_ref, out_ref):
    out_ref[...] = nn_dot(flip_ref[...], grads_ref[...]).astype(BF16)


def share_call(flipped, grads):
    tile = 1024
    return pl.pallas_call(
        share_kernel,
        grid=(flipped.shape[0] // tile,),
        in_specs=[
            pl.BlockSpec((tile, ROWS), lambda i: (i, 0)),
            pl.BlockSpec((ROWS, 3 * CH), lambda i: (0, 0)),
        ],
        out_specs=pl.BlockSpec((tile, 3 * CH), lambda i: (i, 0)),
        out_shape=jax.ShapeDtypeStruct((flipped.shape[0], 3 * CH), BF16),
        compiler_params=params("arbitrary"),
        name="share",
    )(flipped, grads)


def reduce_over(value, axes, count):
    rows, cols = value.shape
    split = value.reshape(count, rows // count, cols)
    got = lax.all_to_all(split, axes, 0, 0, tiled=True)
    return jnp.sum(got.astype(F32), axis=0)


def shards(inputs, proj_weight, filters, out_grad):
    width = inputs.shape[1]
    flat_w = proj_weight.reshape(3 * CH, width)
    fields, send = fields_call(inputs, flat_w, filters, out_grad)
    got = lax.all_to_all(send.reshape(ROWS, 2, ROWS), SEQ, 0, 0, tiled=True)
    flipped = flip_call(inputs)
    conv = conv_call(got.reshape(2 * ROWS, ROWS))
    got = lax.all_to_all(conv.reshape(ROWS, 1, ROWS), SEQ, 0, 0, tiled=True)
    gated, grads, *parts = parts_call(got.reshape(ROWS, ROWS), fields, flat_w)
    arrived = [
        lax.ppermute(parts[k - 1], "chan", [(i, (i + k) % 4) for i in range(4)]) for k in (1, 2, 3)
    ]
    total = parts[3].astype(F32)
    for part in arrived:
        total = total + part.astype(F32)
    input_grad = total.astype(BF16)

    share = share_call(flipped, grads)
    share = reduce_over(share, ("core",), 2).astype(BF16)
    share = reduce_over(share, ("x", "y"), 16).astype(BF16)
    share = reduce_over(share, ("z",), 4)
    scale = 1.0 / math.sqrt(ROWS * ROWS)
    weight_grad = (share * scale).reshape(width // 128, 3, CH).astype(BF16)
    return (gated, weight_grad, input_grad)


def solution(mesh):
    split = Mesh(mesh.devices.reshape(4, 4, 4, 2, 4), SEQ + ("chan",))
    return jax.shard_map(
        shards,
        mesh=split,
        in_specs=(P(SEQ, None), P(None, "chan", None), P(SEQ, "chan"), P(SEQ, "chan")),
        out_specs=(P(SEQ, "chan"), P(SEQ, None, "chan"), P(SEQ, "chan")),
        check_vma=False,
    )
```

time: 989 us -> 130 us (0.13); the launches traced: 978 us -> 130 us
  waiting for transfers between devices: 846 us -> 43.9 us
  starting transfers between devices: 79.2 us -> 34.7 us
  blocking collectives: 0 us -> 30.3 us
  matrix products: 18.8 us -> 0 us
  between operations: 15 us -> 0.9 us
    unnamed x3 -> x0, waiting for transfers between devices: 680 us -> none
    all_to_all x12 -> x3, waiting for transfers between devices: 104 us -> 8.01 us  [the longest x1 7.49 us: shards(): got = lax.all_to_all(conv.reshape(ROWS, 1, ROWS), SEQ, 0, 0, tiled=True)]
    all_to_all x12 -> x3, starting transfers between devices: 79.1 us -> 12.8 us  [the longest x2 6.89 us: reduce_over(): got = lax.all_to_all(split, axes, 0, 0, tiled=True)]
    reduce_scatter x1 -> x0, waiting for transfers between devices: 61.9 us -> none  [shards(): lax.psum_scatter(partial_sum.astype(jnp.bfloat16), 'chan', scatter_dimens...]
    ppermute x0 -> x3, waiting for transfers between devices: none -> 35.9 us  [shards(): lax.ppermute(parts[k - 1], 'chan', [(i, (i + k) % 4) for i in range(4)])]
    all_to_all x0 -> x2, blocking collectives: none -> 30.3 us  [the longest x1 23.8 us: shards(): got = lax.all_to_all(send.reshape(ROWS, 2, ROWS), SEQ, 0, 0, tiled=True)]
    ppermute x0 -> x3, starting transfers between devices: none -> 21.9 us  [shards(): lax.ppermute(parts[k - 1], 'chan', [(i, (i + k) % 4) for i in range(4)])]
    dot_general x35 -> x0, matrix products: 18.8 us -> none  [the longest x32 13.3 us: exact_dot(): jnp.dot(left, right, precision=lax.Precision.HIGHEST, preferred_element_t...]
  transfers between devices with their start and end apart: 14 -> 6, of which waited for: 14 -> 5; matrix products, arithmetic and copies ran while one was open for 2% -> 2% of each run, Pallas kernels for 0% -> 1%
where the time goes in v1:
time: 130 us
  waiting for transfers between devices  43.9 us (34%)
  starting transfers between devices  34.7 us (27%)
  blocking collectives  30.3 us (23%)
  local copies, waits for them, and re-layouts  11.8 us (9%)
  Pallas kernels  6.5 us (5%)
  other arithmetic  1.37 us (1%)
    ppermute x3, waiting for transfers between devices, shards(): lax.ppermute(parts[k - 1], 'chan', [(i, (i + k) % 4) for i in range(4)])  35.9 us
    all_to_all x1, blocking collectives, shards(): got = lax.all_to_all(send.reshape(ROWS, 2, ROWS), SEQ, 0, 0, tiled=True)  23.8 us
    ppermute x3, starting transfers between devices, shards(): lax.ppermute(parts[k - 1], 'chan', [(i, (i + k) % 4) for i in range(4)])  21.9 us
    unnamed x36, local copies, waits for them, and re-layouts  7.63 us
    all_to_all x1, waiting for transfers between devices, shards(): got = lax.all_to_all(conv.reshape(ROWS, 1, ROWS), SEQ, 0, 0, tiled=True)  7.49 us
    all_to_all x2, starting transfers between devices, reduce_over(): got = lax.all_to_all(split, axes, 0, 0, tiled=True)  6.89 us
    all_to_all x1, blocking collectives, reduce_over(): got = lax.all_to_all(split, axes, 0, 0, tiled=True)  6.52 us
    all_to_all x1, starting transfers between devices, shards(): got = lax.all_to_all(conv.reshape(ROWS, 1, ROWS), SEQ, 0, 0, tiled=True)  5.89 us
  transfers between devices with their start and end apart: 6, of which 5 were waited for; matrix products, arithmetic and copies ran while one was open for 2% of the time, Pallas kernels for 1%

profile of v1, /device:TPU:1, one launch (start us, length us, event | category | flops | bytes accessed | tf_op | source)
XLA Modules:
  0.0 129.6 jit_solution(17240658145637341453)
XLA Ops:
  0.6 0.9 copy.41.grad_ref
  1.5 0.9 copy.40.filt_ref
  2.4 1.4 %copy-done = bf16[3,64,4096]{2,1,0:T(8,128)(2,1)S(1)} copy-done((bf16[3,64,4096]{2,1,0:T(8,128)(2,1)S(1)}, bf16[3,64,4096]{2,1,0:T(8,128)(2,1)}, u32[]{:S(2)}) %copy-start) | copy-done | bytes 1572888
  3.8 1.2 copy-done.2
  5.0 1.4 %fields.1 = (bf16[256,128]{1,0:T(8,128)(2,1)S(1)}, bf16[256,128]{1,0:T(8,128)(2,1)S(1)}) custom-call(bf16[128,4096]{1,0:T(8,128)(2,1)S(1)} %copy-done.2, bf16[192,4096]{1,0:T(8,128)(2,1)S(1)} %bitcast.17, f32[128,64]{1,0:T(8,128)S(1)} %copy.40.filt_ref, bf16[128,64]{1,0:T(8,128)(2,1)S(1)} %copy.41.grad_ref), custom_call_target="tpu_custom_call" | custom-call | tf_op jit(solution)/shard_map/fields/pallas_call | solution.py:88
  6.5 23.8 %all_to_all.25 = bf16[128,2,128]{2,1,0:T(2,128)(2,1)S(1)} all-to-all(bf16[128,2,128]{2,1,0:T(2,128)(2,1)S(1)} %bitcast.22), channel_id=1, replica_groups=mesh['z'=4,'x'=4,'y'=4,'core'=2,'chan'=4] {'z','x','y','core'}, dimensions={0} | all-to-all | bytes 131072 | tf_op jit(solution)/shard_map/all_to_all | solution.py:255
  30.3 1.3 conv.1
  31.6 5.9 %all-to-all-start.1 = ((f32[128,1,128]{2,1,0:T(1,128)}), f32[128,1,128]{2,1,0:T(1,128)S(1)}, u32[]{:S(2)}, u32[]{:S(2)}) async-start(f32[128,1,128]{2,1,0:T(1,128)} %bitcast.5), calls=%async_computation.1 | async-start | bytes 131072 | tf_op jit(solution)/shard_map/all_to_all | solution.py:258
  37.5 1.2 copy-done.3
  38.7 1.3 %flip.1 = bf16[2,16,128,128]{3,2,1,0:T(8,128)(2,1)S(1)} custom-call(bf16[128,4096]{1,0:T(8,128)(2,1)S(1)} %copy-done.3), custom_call_target="tpu_custom_call" | custom-call | tf_op jit(solution)/shard_map/flip/pallas_call | solution.py:123
  40.1 7.5 %all-to-all-done.1 = f32[128,1,128]{2,1,0:T(1,128)S(1)} async-done(((f32[128,1,128]{2,1,0:T(1,128)}), f32[128,1,128]{2,1,0:T(1,128)S(1)}, u32[]{:S(2)}, u32[]{:S(2)}) %all-to-all-start.1) | async-done | bytes 65568 | tf_op jit(solution)/shard_map/all_to_all | solution.py:258
  47.6 1.3 %parts.1 = (bf16[128,64]{1,0:T(8,128)(2,1)S(1)}, bf16[128,192]{1,0:T(8,128)(2,1)S(1)}, bf16[128,1024]{1,0:T(8,128)(2,1)S(1)}, bf16[128,1024]{1,0:T(8,128)(2,1)S(...) custom-call(s32[1]{0:T(128)} %bitcast.chan_ref, f32[128,128]{1,0:T(8,128)S(1)} %bitcast.20, ...), custom_call_target="tpu_custom_call" | custom-call | tf_op jit(solution)/shard_map/parts/pallas_call | solution.py:202
  48.9 0.7 copy-done.10
  49.6 1.1 share.1
  50.8 2.3 %copy.43 = bf16[2,2048,192]{1,2,0:T(8,128)(2,1)} copy(bf16[2,2048,192]{2,1,0:T(8,128)(2,1)S(1)} %bitcast.16) | data formatting | bytes 3145728 | tf_op jit(solution)/shard_map/reshape | solution.py:246
  53.1 6.5 %all_to_all.26 = bf16[2,2048,192]{1,2,0:T(8,128)(2,1)S(1)} all-to-all(bf16[2,2048,192]{1,2,0:T(8,128)(2,1)} %copy.43), channel_id=1, replica_groups=mesh['z'=4,'x'=4,'y'=4,'core'=2,'chan'=4] {'core'}, dimensions={0} | all-to-all | bytes 3145728 | tf_op jit(solution)/shard_map/all_to_all | solution.py:247
  59.6 0.4 reduce_sum.33
  60.0 1.1 copy_bitcast_fusion
  61.1 3.6 %all-to-all-start.3 = ((bf16[16,128,192]{1,2,0:T(8,128)(2,1)}), bf16[16,128,192]{1,2,0:T(8,128)(2,1)S(1)}, u32[]{:S(2)}, u32[]{:S(2)}) async-start(bf16[16,128,192]{1,2,0:T(8,128)(2,1)} %copy_bitcast_fusion), calls=%async_computation.3 | async-start | bytes 1572864 | tf_op jit(solution)/shard_map/all_to_all | solution.py:247
  64.7 8.8 %collective-permute-start = (bf16[128,1024]{1,0:T(8,128)(2,1)S(1)}, bf16[128,1024]{1,0:T(8,128)(2,1)S(1)}, u32[]{:S(2)}, u32[]{:S(2)}) collective-permute-start(bf16[128,1024]{1,0:T(8,128)(2,1)S(1)} %copy-done.15), channel_id=1, source_target_pairs={{0,1},{1,2},{2,3},{3,0},{4,5},{5,6},{6,7},{7,4},{8,9},{9,10},{10,1... | collective-permute-start | bytes 786440 | tf_op jit(solution)/shard_map/ppermute | solution.py:261
  73.6 7.9 %collective-permute-start.1 = (bf16[128,1024]{1,0:T(8,128)(2,1)S(1)}, bf16[128,1024]{1,0:T(8,128)(2,1)S(1)}, u32[]{:S(2)}, u32[]{:S(2)}) collective-permute-start(bf16[128,1024]{1,0:T(8,128)(2,1)S(1)} %copy-done.13), channel_id=1, source_target_pairs={{0,2},{1,3},{2,0},{3,1},{4,6},{5,7},{6,4},{7,5},{8,10},{9,11},{10,... | collective-permute-start | bytes 786440 | tf_op jit(solution)/shard_map/ppermute | solution.py:261
  81.5 5.2 %collective-permute-start.2 = (bf16[128,1024]{1,0:T(8,128)(2,1)S(1)}, bf16[128,1024]{1,0:T(8,128)(2,1)S(1)}, u32[]{:S(2)}, u32[]{:S(2)}) collective-permute-start(bf16[128,1024]{1,0:T(8,128)(2,1)S(1)} %copy-done.11), channel_id=1, source_target_pairs={{0,3},{1,0},{2,1},{3,2},{4,7},{5,4},{6,5},{7,6},{8,11},{9,8},{10,9... | collective-permute-start | bytes 786440 | tf_op jit(solution)/shard_map/ppermute | solution.py:261
  86.7 0.7 copy.46
  87.4 0.1 reduce_sum.34
  87.5 0.7 copy.45
  88.3 3.3 %all-to-all-start.4 = ((bf16[4,32,192]{2,1,0:T(8,128)(2,1)}), bf16[4,32,192]{2,1,0:T(8,128)(2,1)S(1)}, u32[]{:S(2)}, u32[]{:S(2)}) async-start(bf16[4,32,192]{2,1,0:T(8,128)(2,1)} %bitcast.9), calls=%async_computation.4 | async-start | bytes 131072 | tf_op jit(solution)/shard_map/all_to_all | solution.py:247
  91.5 1.7 %collective-permute-done = bf16[128,1024]{1,0:T(8,128)(2,1)S(1)} collective-permute-done((bf16[128,1024]{1,0:T(8,128)(2,1)S(1)}, bf16[128,1024]{1,0:T(8,128)(2,1)S(1)}, u32[]{:S(2)}, u32[]{:S(2)}) %collective-permute-start) | collective-permute-done | bytes 262176 | tf_op jit(solution)/shard_map/ppermute | solution.py:261
  93.3 26.1 %collective-permute-done.1 = bf16[128,1024]{1,0:T(8,128)(2,1)S(1)} collective-permute-done((bf16[128,1024]{1,0:T(8,128)(2,1)S(1)}, bf16[128,1024]{1,0:T(8,128)(2,1)S(1)}, u32[]{:S(2)}, u32[]{:S(2)}) %collective-permute-start.1) | collective-permute-done | bytes 262176 | tf_op jit(solution)/shard_map/ppermute | solution.py:261
  119.4 8.0 %collective-permute-done.2 = bf16[128,1024]{1,0:T(8,128)(2,1)S(1)} collective-permute-done((bf16[128,1024]{1,0:T(8,128)(2,1)S(1)}, bf16[128,1024]{1,0:T(8,128)(2,1)S(1)}, u32[]{:S(2)}, u32[]{:S(2)}) %collective-permute-start.2) | collective-permute-done | bytes 262176 | tf_op jit(solution)/shard_map/ppermute | solution.py:261
  127.4 0.9 add_convert_fusion
  128.3 0.5 all-to-all-done.4
  128.9 0.6 copy.47
  (32 shorter events, 0.2 us)
Async XLA Ops:
  0.6 29.7 %copy-start.4 = (bf16[256,256]{1,0:T(8,128)(2,1)S(1)}, bf16[256,256]{1,0:T(8,128)(2,1)}, u32[]{:S(2)}) copy-start(bf16[256,256]{1,0:T(8,128)(2,1)} %constant.27.clone.e2b_ref) | copy-start | bytes 393220
  2.4 1.4 %copy-start = (bf16[3,64,4096]{2,1,0:T(8,128)(2,1)S(1)}, bf16[3,64,4096]{2,1,0:T(8,128)(2,1)}, u32[]{:S(2)}) copy-start(bf16[3,64,4096]{2,1,0:T(8,128)(2,1)} %param.11) | copy-start | bytes 4718596
  3.8 1.2 copy-start.2
  5.0 25.3 %copy-start.5 = (bf16[256,256]{1,0:T(8,128)(2,1)S(1)}, bf16[256,256]{1,0:T(8,128)(2,1)}, u32[]{:S(2)}) copy-start(bf16[256,256]{1,0:T(8,128)(2,1)} %constant.26.clone.e2_ref) | copy-start | bytes 393220
  5.0 25.3 %copy-start.6 = (bf16[128,256]{1,0:T(8,128)(2,1)S(1)}, bf16[128,256]{1,0:T(8,128)(2,1)}, u32[]{:S(2)}) copy-start(bf16[128,256]{1,0:T(8,128)(2,1)} %constant.28.clone.e1b_ref) | copy-start | bytes 196612
  5.0 25.3 %copy-start.7 = (f32[128,128]{1,0:T(8,128)S(1)}, f32[128,128]{1,0:T(8,128)}, u32[]{:S(2)}) copy-start(f32[128,128]{1,0:T(8,128)} %constant.25.clone.twi_ref) | copy-start | bytes 196612
  5.0 25.3 %copy-start.8 = (f32[128,128]{1,0:T(8,128)S(1)}, f32[128,128]{1,0:T(8,128)}, u32[]{:S(2)}) copy-start(f32[128,128]{1,0:T(8,128)} %constant.24.clone.twr_ref) | copy-start | bytes 196612
  5.0 25.3 %copy-start.9 = (bf16[256,128]{1,0:T(8,128)(2,1)S(1)}, bf16[256,128]{1,0:T(8,128)(2,1)}, u32[]{:S(2)}) copy-start(bf16[256,128]{1,0:T(8,128)(2,1)} %constant.23.clone.e1_ref) | copy-start | bytes 196612
  6.5 41.1 %copy-start.1 = (bf16[3,64,4096]{2,1,0:T(8,128)(2,1)S(1)}, bf16[3,64,4096]{2,1,0:T(8,128)(2,1)}, u32[]{:S(2)}) copy-start(bf16[3,64,4096]{2,1,0:T(8,128)(2,1)} %param.11) | copy-start | bytes 4718596
  31.6 16.0 %all-to-all-start.1 = ((f32[128,1,128]{2,1,0:T(1,128)}), f32[128,1,128]{2,1,0:T(1,128)S(1)}, u32[]{:S(2)}, u32[]{:S(2)}) async-start(f32[128,1,128]{2,1,0:T(1,128)} %bitcast.5), calls=%async_computation.1 | async-start | bytes 131072 | tf_op jit(solution)/shard_map/all_to_all | solution.py:258
  37.5 1.2 copy-start.3
  48.9 0.7 copy-start.10
  49.6 1.1 copy-start.12
  49.6 1.1 copy-start.14
  60.0 4.8 %copy-start.15 = (bf16[128,1024]{1,0:T(8,128)(2,1)S(1)}, bf16[128,1024]{1,0:T(8,128)(2,1)}, u32[]{:S(2)}) copy-start(bf16[128,1024]{1,0:T(8,128)(2,1)} %copy-done.14) | copy-start | bytes 786436
  60.0 13.6 %copy-start.13 = (bf16[128,1024]{1,0:T(8,128)(2,1)S(1)}, bf16[128,1024]{1,0:T(8,128)(2,1)}, u32[]{:S(2)}) copy-start(bf16[128,1024]{1,0:T(8,128)(2,1)} %copy-done.12) | copy-start | bytes 786436
  60.0 21.5 %copy-start.11 = (bf16[128,1024]{1,0:T(8,128)(2,1)S(1)}, bf16[128,1024]{1,0:T(8,128)(2,1)}, u32[]{:S(2)}) copy-start(bf16[128,1024]{1,0:T(8,128)(2,1)} %copy-done.10) | copy-start | bytes 786436
  61.1 26.3 %all-to-all-start.3 = ((bf16[16,128,192]{1,2,0:T(8,128)(2,1)}), bf16[16,128,192]{1,2,0:T(8,128)(2,1)S(1)}, u32[]{:S(2)}, u32[]{:S(2)}) async-start(bf16[16,128,192]{1,2,0:T(8,128)(2,1)} %copy_bitcast_fusion), calls=%async_computation.3 | async-start | bytes 1572864 | tf_op jit(solution)/shard_map/all_to_all | solution.py:247
  64.7 28.6 %collective-permute-start = (bf16[128,1024]{1,0:T(8,128)(2,1)S(1)}, bf16[128,1024]{1,0:T(8,128)(2,1)S(1)}, u32[]{:S(2)}, u32[]{:S(2)}) collective-permute-start(bf16[128,1024]{1,0:T(8,128)(2,1)S(1)} %copy-done.15), channel_id=1, source_target_pairs={{0,1},{1,2},{2,3},{3,0},{4,5},{5,6},{6,7},{7,4},{8,9},{9,10},{10,1... | collective-permute-start | bytes 786440 | tf_op jit(solution)/shard_map/ppermute | solution.py:261
  73.6 45.9 %collective-permute-start.1 = (bf16[128,1024]{1,0:T(8,128)(2,1)S(1)}, bf16[128,1024]{1,0:T(8,128)(2,1)S(1)}, u32[]{:S(2)}, u32[]{:S(2)}) collective-permute-start(bf16[128,1024]{1,0:T(8,128)(2,1)S(1)} %copy-done.13), channel_id=1, source_target_pairs={{0,2},{1,3},{2,0},{3,1},{4,6},{5,7},{6,4},{7,5},{8,10},{9,11},{10,... | collective-permute-start | bytes 786440 | tf_op jit(solution)/shard_map/ppermute | solution.py:261
  81.5 45.9 %collective-permute-start.2 = (bf16[128,1024]{1,0:T(8,128)(2,1)S(1)}, bf16[128,1024]{1,0:T(8,128)(2,1)S(1)}, u32[]{:S(2)}, u32[]{:S(2)}) collective-permute-start(bf16[128,1024]{1,0:T(8,128)(2,1)S(1)} %copy-done.11), channel_id=1, source_target_pairs={{0,3},{1,0},{2,1},{3,2},{4,7},{5,4},{6,5},{7,6},{8,11},{9,8},{10,9... | collective-permute-start | bytes 786440 | tf_op jit(solution)/shard_map/ppermute | solution.py:261
  88.3 40.6 %all-to-all-start.4 = ((bf16[4,32,192]{2,1,0:T(8,128)(2,1)}), bf16[4,32,192]{2,1,0:T(8,128)(2,1)S(1)}, u32[]{:S(2)}, u32[]{:S(2)}) async-start(bf16[4,32,192]{2,1,0:T(8,128)(2,1)} %bitcast.9), calls=%async_computation.4 | async-start | bytes 131072 | tf_op jit(solution)/shard_map/all_to_all | solution.py:247

commit v2 on v1

v2 whole, which is shorter than its diff:
```python
import math

import jax
import jax.numpy as jnp
import numpy as np
from jax import lax
from jax.experimental import pallas as pl
from jax.experimental.pallas import tpu as pltpu
from jax.sharding import Mesh, PartitionSpec as P

F32 = jnp.float32
BF16 = jnp.bfloat16
SEQ = ("z", "x", "y", "core")
ROWS = 128
CH = 64
RING = 4
VMEM_LIMIT = 14 * 1024 * 1024
FIRST_LIMIT = 60 * 1024 * 1024


def params(*semantics, limit=VMEM_LIMIT):
    return pltpu.CompilerParams(
        vmem_limit_bytes=limit, dimension_semantics=semantics or None
    )


def nt_dot(left, right):
    return lax.dot_general(left, right, (((1,), (1,)), ((), ())), preferred_element_type=F32)


def tn_dot(left, right):
    return lax.dot_general(left, right, (((0,), (0,)), ((), ())), preferred_element_type=F32)


def nn_dot(left, right):
    return jnp.dot(left, right, preferred_element_type=F32)


def tables():
    length = ROWS * ROWS
    index = np.arange(ROWS)
    first = np.exp(-2j * np.pi * np.outer(index + 0.25, index) / ROWS)
    twist = np.exp(-2j * np.pi * np.outer(index + 0.25, index) / length)
    second = np.exp(-2j * np.pi * np.outer(index, index) / ROWS)
    first_rows = np.concatenate([first.real, first.imag], axis=0)
    second_fwd = np.block([[second.real, second.imag], [-second.imag, second.real]])
    second_bwd = np.block([[second.real, -second.imag], [second.imag, second.real]])
    first_bwd = np.concatenate([first.real.T, first.imag.T], axis=1) / length
    as_bf16 = lambda x: jnp.asarray(x, dtype=BF16)
    as_f32 = lambda x: jnp.asarray(x, dtype=F32)
    return (
        as_bf16(first_rows),
        as_f32(twist.real),
        as_f32(twist.imag),
        as_bf16(second_fwd),
        as_bf16(second_bwd),
        as_bf16(first_bwd),
    )


def fields_kernel(
    x_hbm, w_hbm, filt_hbm, grad_hbm, fields_ref, send_ref, x_ref, w_ref, filt_ref, grad_ref, scratch, sems
):
    parts, tile = x_ref.shape[0], x_ref.shape[2]
    small = [
        pltpu.make_async_copy(filt_hbm, filt_ref, sems.at[0]),
        pltpu.make_async_copy(grad_hbm, grad_ref, sems.at[1]),
    ]
    copies = []
    for part in range(parts):
        cols = slice(part * tile, (part + 1) * tile)
        copies.append(
            (
                pltpu.make_async_copy(x_hbm.at[:, cols], x_ref.at[part], sems.at[2 + 2 * part]),
                pltpu.make_async_copy(w_hbm.at[:, cols], w_ref.at[part], sems.at[3 + 2 * part]),
            )
        )
    for pair in copies:
        for copy in pair:
            copy.start()
    for copy in small:
        copy.start()
    acc = jnp.zeros((3 * CH, ROWS), F32)
    for part, pair in enumerate(copies):
        for copy in pair:
            copy.wait()
        acc += nt_dot(w_ref[part], x_ref[part])
    for copy in small:
        copy.wait()
    fields = acc.astype(BF16)
    grad_t = grad_ref[...]
    fields_ref[0 : 3 * CH, :] = fields
    fields_ref[3 * CH : 4 * CH, :] = grad_t
    query = fields[0:CH].astype(F32)
    key = fields[CH : 2 * CH].astype(F32)
    value = fields[2 * CH : 3 * CH].astype(F32)
    filt_t = filt_ref[...]
    scratch[pl.ds(0, CH, stride=4), :] = key * value
    scratch[pl.ds(1, CH, stride=4), :] = filt_t
    scratch[pl.ds(2, CH, stride=4), :] = grad_t.astype(F32) * query
    scratch[pl.ds(3, CH, stride=4), :] = filt_t
    send_ref[...] = scratch[...].astype(BF16)


def fields_call(inputs, flat_w, filters_t, grad_t):
    tile = 1024
    parts = inputs.shape[1] // tile
    return pl.pallas_call(
        fields_kernel,
        in_specs=[pl.BlockSpec(memory_space=pl.ANY)] * 4,
        out_shape=[jax.ShapeDtypeStruct((4 * CH, ROWS), BF16)] * 2,
        scratch_shapes=[
            pltpu.VMEM((parts, ROWS, tile), BF16),
            pltpu.VMEM((parts, 3 * CH, tile), BF16),
            pltpu.VMEM((CH, ROWS), F32),
            pltpu.VMEM((CH, ROWS), BF16),
            pltpu.VMEM((4 * CH, ROWS), F32),
            pltpu.SemaphoreType.DMA((2 + 2 * parts,)),
        ],
        compiler_params=params(limit=FIRST_LIMIT),
        name="fields",
    )(inputs, flat_w, filters_t, grad_t)


def flip_kernel(x_ref, other_ref, out_ref, scratch):
    core = lax.axis_index("core")
    for place, ref in enumerate((x_ref, other_ref)):
        scratch[...] = ref[...].astype(F32).T
        for block in range(out_ref.shape[0]):
            start = pl.multiple_of(64 * block + 32 * core, 32)
            rows = scratch[pl.ds(start, 32), :].astype(BF16)
            out_ref[block, 0, :, ROWS * place : ROWS * (place + 1)] = rows


def flip_call(inputs, other_inputs):
    tile = 1024
    steps = inputs.shape[1] // tile
    return pl.pallas_call(
        flip_kernel,
        grid=(steps,),
        in_specs=[pl.BlockSpec((ROWS, tile), lambda i: (0, i))] * 2,
        out_specs=pl.BlockSpec((tile // 64, 1, 32, 2 * ROWS), lambda i: (0, i, 0, 0)),
        out_shape=jax.ShapeDtypeStruct((tile // 64, steps, 32, 2 * ROWS), BF16),
        scratch_shapes=[pltpu.VMEM((tile, ROWS), F32)],
        compiler_params=params("arbitrary"),
        name="flip",
    )(inputs, other_inputs)


def conv_kernel(got_ref, e1_ref, twr_ref, twi_ref, e2_ref, e2b_ref, e1b_ref, out_ref, scratch, spread):
    sign = jnp.where(lax.axis_index("core") == 0, 1.0, -1.0).astype(F32)
    scratch[...] = got_ref[...].astype(F32)
    signal = scratch[pl.ds(0, ROWS, stride=2), :].astype(BF16)
    filt = scratch[pl.ds(1, ROWS, stride=2), :].astype(BF16)
    twr, twi = twr_ref[...], twi_ref[...]

    both = nn_dot(e1_ref[...], jnp.concatenate([signal, filt], axis=1))

    def twisted(part):
        re, im = part[0:ROWS], part[ROWS:]
        return jnp.concatenate([re * twr - im * twi, re * twi + im * twr], axis=1)

    mid = jnp.concatenate([twisted(both[:, 0:ROWS]), twisted(both[:, ROWS:])], axis=0)
    spec = nn_dot(mid.astype(BF16), e2_ref[...])
    sig_re, sig_im = spec[0:ROWS, 0:ROWS], spec[0:ROWS, ROWS:]
    fil_re, fil_im = spec[ROWS:, 0:ROWS], spec[ROWS:, ROWS:] * sign
    prod_re = sig_re * fil_re - sig_im * fil_im
    prod_im = sig_re * fil_im + sig_im * fil_re
    prod = jnp.concatenate([prod_re, prod_im], axis=1).astype(BF16)
    back = nn_dot(prod, e2b_ref[...])
    re, im = back[:, 0:ROWS], back[:, ROWS:]
    stack = jnp.concatenate([re * twr + im * twi, im * twr - re * twi], axis=0).astype(BF16)
    result = nn_dot(e1b_ref[...], stack)
    half = ROWS // 2
    spread[0:ROWS, :] = result
    even = spread[pl.ds(0, half, stride=2), :]
    odd = spread[pl.ds(1, half, stride=2), :]
    for place, rows in enumerate((even, odd, odd, even)):
        spread[pl.ds(place, half, stride=4), :] = rows
    out_ref[...] = spread[...].astype(BF16)


def conv_call(got):
    return pl.pallas_call(
        conv_kernel,
        out_shape=jax.ShapeDtypeStruct((2 * ROWS, ROWS), BF16),
        scratch_shapes=[pltpu.VMEM((2 * ROWS, ROWS), F32)] * 2,
        compiler_params=params(),
        name="conv",
    )(got, *tables())


def conv_of(scratch, block):
    conv = scratch[pl.ds(block, CH, stride=4), :]
    grad_mixed = scratch[pl.ds(2 + block, CH, stride=4), :]
    return conv, grad_mixed


def grads_of(conv, grad_mixed, fields):
    fields = fields.astype(F32)
    key, value = fields[CH : 2 * CH], fields[2 * CH : 3 * CH]
    grad = fields[3 * CH :]
    grads = jnp.concatenate([grad * conv, grad_mixed * value, grad_mixed * key], axis=0)
    return grads.T.astype(BF16)


def parts_kernel(chan_ref, got_ref, fields_ref, w_ref, gated_ref, grads_ref, *rest):
    part_refs, scratch = rest[:-1], rest[-1]

    @pl.when(pl.program_id(0) == 0)
    def _():
        scratch[...] = got_ref[...].astype(F32)
        conv, grad_mixed = conv_of(scratch, 0)
        fields = fields_ref[...]
        gated_ref[...] = (fields[0:CH].astype(F32) * conv).astype(BF16)
        grads_ref[...] = grads_of(conv, grad_mixed, fields)

    part = nn_dot(grads_ref[...], w_ref[...]).astype(BF16)
    for place, part_ref in enumerate(part_refs):

        @pl.when(pl.program_id(0) == place)
        def _(part_ref=part_ref):
            part_ref[...] = part


def parts_call(chan, got, fields, flat_w):
    slab = flat_w.shape[1] // RING
    whole = lambda shape: pl.BlockSpec(shape, lambda i, chan: (0, 0))
    shift = lambda i: jnp.where(i == 0, 2, jnp.where(i == 3, 0, 2 * i - 1))
    return pl.pallas_call(
        parts_kernel,
        grid_spec=pltpu.PrefetchScalarGridSpec(
            num_scalar_prefetch=1,
            grid=(RING,),
            in_specs=[
                whole((2 * ROWS, ROWS)),
                whole((4 * CH, ROWS)),
                pl.BlockSpec(
                    (3 * CH, slab), lambda i, chan: (0, lax.rem(chan[0] + shift(i), RING))
                ),
            ],
            out_specs=[whole((CH, ROWS)), whole((ROWS, 3 * CH))] + [whole((ROWS, slab))] * RING,
            scratch_shapes=[pltpu.VMEM((2 * ROWS, ROWS), F32)],
        ),
        out_shape=[
            jax.ShapeDtypeStruct((CH, ROWS), BF16),
            jax.ShapeDtypeStruct((ROWS, 3 * CH), BF16),
        ]
        + [jax.ShapeDtypeStruct((ROWS, slab), BF16)] * RING,
        compiler_params=params("arbitrary"),
        name="parts",
    )(chan, got, fields, flat_w)


def share_kernel(before_ref, got_ref, own_ref, other_ref, flipped_ref, out_ref, scratch, grads):
    del before_ref

    @pl.when(pl.program_id(0) == 0)
    def _():
        scratch[...] = got_ref[...].astype(F32)
        for block, ref in enumerate((own_ref, other_ref)):
            grads[ROWS * block : ROWS * (block + 1), :] = grads_of(
                *conv_of(scratch, block), ref[...]
            )

    blocks = flipped_ref.shape[0]
    total = nn_dot(flipped_ref[...].reshape(blocks * 32, 2 * ROWS), grads[...])
    out_ref[:, 0:32, :] = total[:, 0:ROWS].reshape(blocks, 32, ROWS).astype(BF16)
    last = total[:, ROWS:].reshape(blocks, 32, CH)
    out_ref[:, 32:48, :] = jnp.concatenate([last[:, 0:16], last[:, 16:32]], axis=2).astype(BF16)


def share_call(before, got, fields, other_fields, flipped):
    planes, steps = flipped.shape[:2]
    tile = 16
    whole = lambda shape: pl.BlockSpec(shape, lambda i: (0, 0))
    flipped = flipped.reshape(planes * steps, 32, 2 * ROWS)
    out = pl.pallas_call(
        share_kernel,
        grid=(planes * steps // tile,),
        in_specs=[
            pl.BlockSpec(memory_space=pl.ANY),
            whole((2 * ROWS, ROWS)),
            whole((4 * CH, ROWS)),
            whole((4 * CH, ROWS)),
            pl.BlockSpec((tile, 32, 2 * ROWS), lambda i: (i, 0, 0)),
        ],
        out_specs=pl.BlockSpec((tile, 48, ROWS), lambda i: (i, 0, 0)),
        out_shape=jax.ShapeDtypeStruct((planes * steps, 48, ROWS), BF16),
        scratch_shapes=[
            pltpu.VMEM((2 * ROWS, ROWS), F32),
            pltpu.VMEM((2 * ROWS, 3 * CH), BF16),
        ],
        compiler_params=params("arbitrary"),
        name="share",
    )(before, got, fields, other_fields, flipped)
    return out.reshape(planes, steps, 48, ROWS)


def stage_kernel(got_ref, out_ref):
    out_ref[...] = jnp.sum(got_ref[...].astype(F32), axis=0).astype(BF16)


def stage_call(got):
    return pl.pallas_call(
        stage_kernel,
        out_shape=jax.ShapeDtypeStruct(got.shape[1:], BF16),
        compiler_params=params(),
        name="stage",
    )(got)


def total_kernel(got_ref, out_ref):
    total = jnp.sum(got_ref[...].astype(F32), axis=0) * (1.0 / math.sqrt(ROWS * ROWS))
    total = total.astype(BF16)
    out_ref[0, :, :] = total[0:32, 0:CH]
    out_ref[1, :, :] = total[0:32, CH:]
    out_ref[2, 0:16, :] = total[32:48, 0:CH]
    out_ref[2, 16:32, :] = total[32:48, CH:]


def total_call(got):
    return pl.pallas_call(
        total_kernel,
        out_shape=jax.ShapeDtypeStruct((3, 32, CH), BF16),
        compiler_params=params(),
        name="total",
    )(got)


def turned(value, axis, shift):
    size = lax.axis_size(axis)
    return lax.ppermute(value, axis, [(i, (i + shift) % size) for i in range(size)])


def shards(inputs, proj_weight, filters, out_grad):
    width = inputs.shape[1]
    flat_w = proj_weight.reshape(3 * CH, width)
    chan = lax.axis_index("chan").reshape(1)
    fields, send = fields_call(inputs, flat_w, filters.T, out_grad.T)
    late_inputs, fields = lax.optimization_barrier((inputs, fields))
    other_inputs = turned(late_inputs, "core", 1)
    other_fields = turned(fields, "core", 1)
    got = lax.all_to_all(send.reshape(ROWS, 2, ROWS), SEQ, 0, 0, tiled=True)
    got, other_inputs, other_fields = lax.optimization_barrier((got, other_inputs, other_fields))
    flipped = flip_call(inputs, other_inputs)
    conv = conv_call(got.reshape(2 * ROWS, ROWS))
    got = lax.all_to_all(conv.reshape(ROWS, 2, ROWS), SEQ, 0, 0, tiled=True)
    got = got.reshape(2 * ROWS, ROWS)
    gated, grads, *parts = parts_call(chan, got, fields, flat_w)
    arrived = [turned(part, "chan", shift) for shift, part in zip((2, 1, 3), parts)]

    def weights(_, before):
        share = share_call(before, got, fields, other_fields, flipped)
        share = stage_call(lax.all_to_all(share, ("x", "y"), 0, 0, tiled=True))
        share = lax.all_to_all(share, "z", 0, 0, tiled=True)
        return total_call(share)

    once = jnp.minimum(lax.axis_index("x") + 1, 1)
    weight_grad = lax.fori_loop(0, once, weights, jnp.zeros((3, width // ROWS, CH), BF16))
    weight_grad, own = lax.optimization_barrier((weight_grad, parts[3]))
    weight_grad = jnp.transpose(weight_grad, (1, 0, 2))
    total = own.astype(F32)
    for part in arrived:
        total = total + part.astype(F32)
    input_grad = total.astype(BF16)
    return (gated.T, weight_grad, input_grad)


def solution(mesh):
    split = Mesh(mesh.devices.reshape(4, 4, 4, 2, 4), SEQ + ("chan",))
    return jax.shard_map(
        shards,
        mesh=split,
        in_specs=(P(SEQ, None), P(None, "chan", None), P(SEQ, "chan"), P(SEQ, "chan")),
        out_specs=(P(SEQ, "chan"), P(SEQ, None, "chan"), P(SEQ, "chan")),
        check_vma=False,
    )
```

time: 130 us -> 112 us (0.86)
  blocking collectives: 30.3 us -> 14.9 us
  starting transfers between devices: 34.7 us -> 49.8 us
  local copies, waits for them, and re-layouts: 11.8 us -> 0.07 us
  waiting for transfers between devices: 43.9 us -> 32.2 us
  Pallas kernels: 6.5 us -> 11.8 us
    ppermute x3 -> x5, waiting for transfers between devices: 35.9 us -> 0.89 us  [turned(): lax.ppermute(value, axis, [(i, (i + shift) % size) for i in range(size)])]
    all_to_all x3, waiting for transfers between devices: 8.01 us -> 31.3 us  [the longest x1 15 us: weights(): share = lax.all_to_all(share, 'z', 0, 0, tiled=True)]
    all_to_all x2 -> x1, blocking collectives: 30.3 us -> 14.9 us  [weights(): share = stage_call(lax.all_to_all(share, ('x', 'y'), 0, 0, tiled=True))]
    ppermute x3 -> x5, starting transfers between devices: 21.9 us -> 33.5 us  [turned(): lax.ppermute(value, axis, [(i, (i + shift) % size) for i in range(size)])]
    unnamed x36 -> x22, local copies, waits for them, and re-layouts: 7.63 us -> 0.06 us
    pallas_call x4 -> x6, Pallas kernels: 5.15 us -> 9.77 us  [the longest x1 3.32 us: fields_call(): pl.pallas_call(fields_kernel, in_specs=[pl.BlockSpec(memory_space=pl.ANY)...]
    all_to_all x3, starting transfers between devices: 12.8 us -> 16.2 us  [the longest x1 7.08 us: shards(): got = lax.all_to_all(send.reshape(ROWS, 2, ROWS), SEQ, 0, 0, tiled=True)]
    reshape x2 -> x0, local copies, waits for them, and re-layouts: 3.38 us -> none  [reduce_over(): split = value.reshape(count, rows // count, cols)]
  transfers between devices with their start and end apart: 6 -> 8, of which waited for: 5 -> 4; matrix products, arithmetic and copies ran while one was open for 2% -> 0% of each run, Pallas kernels for 1% -> 5%
where the time goes in v2:
time: 112 us
  starting transfers between devices  49.8 us (44%)
  waiting for transfers between devices  32.2 us (29%)
  blocking collectives  14.9 us (13%)
  Pallas kernels  11.8 us (11%)
  other arithmetic  1.9 us (2%)
    ppermute x5, starting transfers between devices, turned(): lax.ppermute(value, axis, [(i, (i + shift) % size) for i in range(size)])  33.5 us
    all_to_all x1, waiting for transfers between devices, weights(): share = lax.all_to_all(share, 'z', 0, 0, tiled=True)  15 us
    all_to_all x1, blocking collectives, weights(): share = stage_call(lax.all_to_all(share, ('x', 'y'), 0, 0, tiled=True))  14.9 us
    all_to_all x1, waiting for transfers between devices, shards(): got = lax.all_to_all(conv.reshape(ROWS, 2, ROWS), SEQ, 0, 0, tiled=True)  10.1 us
    all_to_all x1, starting transfers between devices, shards(): got = lax.all_to_all(send.reshape(ROWS, 2, ROWS), SEQ, 0, 0, tiled=True)  7.08 us
    all_to_all x1, waiting for transfers between devices, shards(): got = lax.all_to_all(send.reshape(ROWS, 2, ROWS), SEQ, 0, 0, tiled=True)  6.27 us
    all_to_all x1, starting transfers between devices, shards(): got = lax.all_to_all(conv.reshape(ROWS, 2, ROWS), SEQ, 0, 0, tiled=True)  5.89 us
    pallas_call x1, Pallas kernels, fields_call(): pl.pallas_call(fields_kernel, in_specs=[pl.BlockSpec(memory_space=pl.ANY)...  3.32 us
  transfers between devices with their start and end apart: 8, of which 4 were waited for; matrix products, arithmetic and copies ran while one was open for 0% of the time, Pallas kernels for 5%

profile of v2, /device:TPU:1, one launch (start us, length us, event | category | flops | bytes accessed | tf_op | source)
XLA Modules:
  0.0 111.5 jit_solution(16261824453812462552)
XLA Ops:
  0.6 0.0 copy-start.4
  0.6 0.0 copy-start.2
  0.7 0.0 copy-start.3
  0.7 0.0 copy-start.5
  0.7 0.0 copy-start.6
  0.7 0.0 copy-start.7
  0.7 3.3 %fields.1 = (bf16[256,128]{1,0:T(8,128)(2,1)S(1)}, bf16[256,128]{1,0:T(8,128)(2,1)}) custom-call(bf16[128,4096]{1,0:T(8,128)(2,1)} %x_ref.1, bf16[192,4096]{1,0:T(8,128)(2,1)} %bitcast.17, f32[64,128]{1,0:T(8,128)} %bitcast.25, bf16[64,128]{1,0:T(8,128)(2,1)} %bitcast.26), custom_call_target="tpu_custom_call" | custom-call | tf_op jit(solution)/shard_map/fields/pallas_call | solution.py:108
  4.1 8.8 %collective-permute-start = (bf16[128,4096]{1,0:T(8,128)(2,1)S(1)}, bf16[128,4096]{1,0:T(8,128)(2,1)}, u32[]{:S(2)}, u32[]{:S(2)}) collective-permute-start(bf16[128,4096]{1,0:T(8,128)(2,1)S(1)} %copy-done.1), channel_id=1, source_target_pairs={{0,4},{4,0},{1,5},{5,1},{2,6},{6,2},{3,7},{7,3},{8,12},{12,8},{9,1... | collective-permute-start | bytes 3145736 | tf_op jit(solution)/shard_map/ppermute | solution.py:333
  12.9 7.1 %all-to-all-start.2 = ((bf16[128,2,128]{2,1,0:T(2,128)(2,1)}), bf16[128,2,128]{2,1,0:T(2,128)(2,1)S(1)}, u32[]{:S(2)}, u32[]{:S(2)}) async-start(bf16[128,2,128]{2,1,0:T(2,128)(2,1)} %bitcast.24), calls=%async_computation.2 | async-start | bytes 131072 | tf_op jit(solution)/shard_map/all_to_all | solution.py:344
  19.9 2.8 %collective-permute-start.1 = (bf16[256,128]{1,0:T(8,128)(2,1)S(1)}, bf16[256,128]{1,0:T(8,128)(2,1)S(1)}, u32[]{:S(2)}, u32[]{:S(2)}) collective-permute-start(bf16[256,128]{1,0:T(8,128)(2,1)S(1)} %get-tuple-element.133.fields_ref), channel_id=1, source_target_pairs={{0,4},{4,0},{1,5},{5,1},{2,6},{6,2},{3,7},{7,3},{8,12},{12,8},{9,1... | collective-permute-start | bytes 196616 | tf_op jit(solution)/shard_map/ppermute | solution.py:333
  22.8 0.9 collective-permute-done.1
  23.6 6.3 %all-to-all-done.2 = bf16[128,2,128]{2,1,0:T(2,128)(2,1)S(1)} async-done(((bf16[128,2,128]{2,1,0:T(2,128)(2,1)}), bf16[128,2,128]{2,1,0:T(2,128)(2,1)S(1)}, u32[]{:S(2)}, u32[]{:S(2)}) %all-to-all-start.2) | async-done | bytes 65568 | tf_op jit(solution)/shard_map/all_to_all | solution.py:344
  29.9 0.0 collective-permute-done.other_ref
  30.0 1.3 %conv.1 = bf16[256,128]{1,0:T(8,128)(2,1)} custom-call(bf16[256,128]{1,0:T(8,128)(2,1)S(1)} %bitcast.19, bf16[256,128]{1,0:T(8,128)(2,1)S(1)} %copy-done.7, f32[128,128]{1,0:T(8,128)S(1)} %copy-done.6, f32[128,128]{1,0:T(8,128)S(1)} %copy-done.5, bf16[256,256]{1,0:T(8,128)(2,1)S(1)} %copy-done.3, bf16[256,256]{1,0:T(8,128)(2,1)S(1)} %copy-done.2, ...), custom_call_target="tpu_custom_call" | custom-call | tf_op jit(solution)/shard_map/conv/pallas_call | solution.py:184
  31.2 5.9 %all-to-all-start.3 = ((bf16[128,2,128]{2,1,0:T(2,128)(2,1)}), bf16[128,2,128]{2,1,0:T(2,128)(2,1)S(1)}, u32[]{:S(2)}, u32[]{:S(2)}) async-start(bf16[128,2,128]{2,1,0:T(2,128)(2,1)} %bitcast.8), calls=%async_computation.3 | async-start | bytes 131072 | tf_op jit(solution)/shard_map/all_to_all | solution.py:348
  37.1 10.1 %all-to-all-done.3 = bf16[128,2,128]{2,1,0:T(2,128)(2,1)S(1)} async-done(((bf16[128,2,128]{2,1,0:T(2,128)(2,1)}), bf16[128,2,128]{2,1,0:T(2,128)(2,1)S(1)}, u32[]{:S(2)}, u32[]{:S(2)}) %all-to-all-start.3) | async-done | bytes 65568 | tf_op jit(solution)/shard_map/all_to_all | solution.py:348
  47.2 2.1 %parts.1 = (bf16[64,128]{1,0:T(8,128)(2,1)}, bf16[128,192]{1,0:T(8,128)(2,1)}, bf16[128,1024]{1,0:T(8,128)(2,1)}, bf16[128,1024]{1,0:T(8,128)(2,1)S(1)}, bf16[12...) custom-call(s32[1]{0:T(128)} %bitcast.2.chan_ref, bf16[256,128]{1,0:T(8,128)(2,1)S(1)} %bitcast.21, ...), custom_call_target="tpu_custom_call" | custom-call | tf_op jit(solution)/shard_map/parts/pallas_call | solution.py:230
  49.3 12.7 %collective-permute-start.2 = (bf16[128,1024]{1,0:T(8,128)(2,1)}, bf16[128,1024]{1,0:T(8,128)(2,1)S(1)}, u32[]{:S(2)}, u32[]{:S(2)}) collective-permute-start(bf16[128,1024]{1,0:T(8,128)(2,1)} %get-tuple-element.67), channel_id=1, source_target_pairs={{0,2},{1,3},{2,0},{3,1},{4,6},{5,7},{6,4},{7,5},{8,10},{9,11},{10,... | collective-permute-start | bytes 786440 | tf_op jit(solution)/shard_map/ppermute | solution.py:333
  62.1 4.0 %collective-permute-start.3 = (bf16[128,1024]{1,0:T(8,128)(2,1)S(1)}, bf16[128,1024]{1,0:T(8,128)(2,1)}, u32[]{:S(2)}, u32[]{:S(2)}) collective-permute-start(bf16[128,1024]{1,0:T(8,128)(2,1)S(1)} %get-tuple-element.68), channel_id=1, source_target_pairs={{0,1},{1,2},{2,3},{3,0},{4,5},{5,6},{6,7},{7,4},{8,9},{9,10},{10,1... | collective-permute-start | bytes 786440 | tf_op jit(solution)/shard_map/ppermute | solution.py:333
  66.1 5.2 %collective-permute-start.4 = (bf16[128,1024]{1,0:T(8,128)(2,1)S(1)}, bf16[128,1024]{1,0:T(8,128)(2,1)}, u32[]{:S(2)}, u32[]{:S(2)}) collective-permute-start(bf16[128,1024]{1,0:T(8,128)(2,1)S(1)} %get-tuple-element.69), channel_id=1, source_target_pairs={{0,3},{1,0},{2,1},{3,2},{4,7},{5,4},{6,5},{7,6},{8,11},{9,8},{10,9... | collective-permute-start | bytes 786440 | tf_op jit(solution)/shard_map/ppermute | solution.py:333
  71.3 3.0 %flip.1 = bf16[16,4,32,256]{3,2,1,0:T(8,128)(2,1)S(1)} custom-call(bf16[128,4096]{1,0:T(8,128)(2,1)S(1)} %copy-done.1, bf16[128,4096]{1,0:T(8,128)(2,1)} %collective-permute-done.other_ref), custom_call_target="tpu_custom_call" | custom-call | tf_op jit(solution)/shard_map/flip/pallas_call | solution.py:138
  74.3 35.3 %while.10 = (s32[]{:T(128)}, bf16[3,32,64]{2,1,0:T(8,128)(2,1)S(1)}, s32[]{:T(128)}, bf16[16,4,32,256]{3,2,1,0:T(8,128)(2,1)S(1)}, bf16[256,128]{1,0:T(8,128)(2,...) while((s32[]{:T(128)}, bf16[3,32,64]{2,1,0:T(8,128)(2,1)S(1)}, ...), condition=%wide.region_1.0_spmd, body=%wide.region_0.0_spmd.sunk | while | flops 2 | bytes 1720437 | solution.py:360
  74.3 1.3 %share.1 = bf16[64,48,128]{2,1,0:T(8,128)(2,1)S(1)} custom-call(bf16[3,32,64]{2,1,0:T(8,128)(2,1)S(1)} %get-tuple-element.137.before_ref, bf16[256,128]{1,0:T(8,128)(2,1)S(1)} %get-tuple-element.148.got_ref, bf16[256,128]{1,0:T(8,128)(2,1)S(1)} %get-tuple-element.149.own_ref, bf16[256,128]{1,0:T(8,128)(2,1)S(1)} %get-tuple-element.150.other_ref, ...), custom_call_target="tpu_custom_call" | custom-call | tf_op jit(solution)/shard_map/while/body/share/pallas_call | solution.py:278
  75.7 14.9 %all_to_all.22.got_ref = bf16[16,4,48,128]{3,2,1,0:T(8,128)(2,1)S(1)} all-to-all(bf16[16,4,48,128]{3,2,1,0:T(8,128)(2,1)S(1)} %bitcast.16), channel_id=1, replica_groups=mesh['z'=4,'x'=4,'y'=4,'core'=2,'chan'=4] {'x','y'}, dimensions={0} | all-to-all | bytes 1572864 | tf_op jit(solution)/shard_map/while/body/all_to_all | solution.py:355
  90.5 0.7 stage.1
  91.3 3.3 %all-to-all-start.1 = ((bf16[4,48,128]{2,1,0:T(8,128)(2,1)}), bf16[4,48,128]{2,1,0:T(8,128)(2,1)S(1)}, u32[]{:S(2)}, u32[]{:S(2)}) async-start(bf16[4,48,128]{2,1,0:T(8,128)(2,1)} %stage.1), calls=%async_computation.1 | async-start | bytes 98304 | tf_op jit(solution)/shard_map/while/body/all_to_all | solution.py:356
  94.6 15.0 %all-to-all-done.1.got_ref = bf16[4,48,128]{2,1,0:T(8,128)(2,1)S(1)} async-done(((bf16[4,48,128]{2,1,0:T(8,128)(2,1)}), bf16[4,48,128]{2,1,0:T(8,128)(2,1)S(1)}, u32[]{:S(2)}, u32[]{:S(2)}) %all-to-all-start.1) | async-done | bytes 49184 | tf_op jit(solution)/shard_map/while/body/all_to_all | solution.py:356
  109.5 0.1 total.1
  109.6 0.0 collective-permute-done.2
  109.6 0.0 collective-permute-done.3
  109.6 0.0 collective-permute-done.4
  109.6 1.9 %add_convert_fusion = bf16[128,1024]{1,0:T(8,128)(2,1)} fusion(bf16[128,1024]{1,0:T(8,128)(2,1)} %collective-permute-done.4, bf16[128,1024]{1,0:T(8,128)(2,1)} %collective-permute-done.3, bf16[128,1024]{1,0:T(8,128)(2,1)S(1)} %collective-permute-done.2, bf16[128,1024]{1,0:T(8,128)(2,1)S(1)} %get-tuple-element.66), kind=kLoop, calls=%fused_computation | loop fusion | flops 1048576 | bytes 1310720 | tf_op jit(solution)/shard_map/convert_element_type | solution.py:366
  (17 shorter events, 0.0 us)
Async XLA Ops:
  0.6 29.3 %copy-start.4 = (bf16[128,256]{1,0:T(8,128)(2,1)S(1)}, bf16[128,256]{1,0:T(8,128)(2,1)}, u32[]{:S(2)}) copy-start(bf16[128,256]{1,0:T(8,128)(2,1)} %constant.33.clone.e1b_ref) | copy-start | bytes 196612
  0.6 29.3 %copy-start.2 = (bf16[256,256]{1,0:T(8,128)(2,1)S(1)}, bf16[256,256]{1,0:T(8,128)(2,1)}, u32[]{:S(2)}) copy-start(bf16[256,256]{1,0:T(8,128)(2,1)} %constant.32.clone.e2b_ref) | copy-start | bytes 393220
  0.7 29.3 %copy-start.3 = (bf16[256,256]{1,0:T(8,128)(2,1)S(1)}, bf16[256,256]{1,0:T(8,128)(2,1)}, u32[]{:S(2)}) copy-start(bf16[256,256]{1,0:T(8,128)(2,1)} %constant.31.clone.e2_ref) | copy-start | bytes 393220
  0.7 29.3 %copy-start.5 = (f32[128,128]{1,0:T(8,128)S(1)}, f32[128,128]{1,0:T(8,128)}, u32[]{:S(2)}) copy-start(f32[128,128]{1,0:T(8,128)} %constant.30.clone.twi_ref) | copy-start | bytes 196612
  0.7 29.3 %copy-start.6 = (f32[128,128]{1,0:T(8,128)S(1)}, f32[128,128]{1,0:T(8,128)}, u32[]{:S(2)}) copy-start(f32[128,128]{1,0:T(8,128)} %constant.29.clone.twr_ref) | copy-start | bytes 196612
  0.7 29.3 %copy-start.7 = (bf16[256,128]{1,0:T(8,128)(2,1)S(1)}, bf16[256,128]{1,0:T(8,128)(2,1)}, u32[]{:S(2)}) copy-start(bf16[256,128]{1,0:T(8,128)(2,1)} %constant.28.clone.e1_ref) | copy-start | bytes 196612
  0.7 3.3 %copy-start.1 = (bf16[128,4096]{1,0:T(8,128)(2,1)S(1)}, bf16[128,4096]{1,0:T(8,128)(2,1)}, u32[]{:S(2)}) copy-start(bf16[128,4096]{1,0:T(8,128)(2,1)} %x_ref.1) | copy-start | bytes 3145732
  0.7 46.5 %copy-start = (bf16[3,64,4096]{2,1,0:T(8,128)(2,1)S(1)}, bf16[3,64,4096]{2,1,0:T(8,128)(2,1)}, u32[]{:S(2)}) copy-start(bf16[3,64,4096]{2,1,0:T(8,128)(2,1)} %param.13) | copy-start | bytes 4718596
  4.1 25.9 %collective-permute-start = (bf16[128,4096]{1,0:T(8,128)(2,1)S(1)}, bf16[128,4096]{1,0:T(8,128)(2,1)}, u32[]{:S(2)}, u32[]{:S(2)}) collective-permute-start(bf16[128,4096]{1,0:T(8,128)(2,1)S(1)} %copy-done.1), channel_id=1, source_target_pairs={{0,4},{4,0},{1,5},{5,1},{2,6},{6,2},{3,7},{7,3},{8,12},{12,8},{9,1... | collective-permute-start | bytes 3145736 | tf_op jit(solution)/shard_map/ppermute | solution.py:333
  12.9 17.1 %all-to-all-start.2 = ((bf16[128,2,128]{2,1,0:T(2,128)(2,1)}), bf16[128,2,128]{2,1,0:T(2,128)(2,1)S(1)}, u32[]{:S(2)}, u32[]{:S(2)}) async-start(bf16[128,2,128]{2,1,0:T(2,128)(2,1)} %bitcast.24), calls=%async_computation.2 | async-start | bytes 131072 | tf_op jit(solution)/shard_map/all_to_all | solution.py:344
  19.9 3.7 %collective-permute-start.1 = (bf16[256,128]{1,0:T(8,128)(2,1)S(1)}, bf16[256,128]{1,0:T(8,128)(2,1)S(1)}, u32[]{:S(2)}, u32[]{:S(2)}) collective-permute-start(bf16[256,128]{1,0:T(8,128)(2,1)S(1)} %get-tuple-element.133.fields_ref), channel_id=1, source_target_pairs={{0,4},{4,0},{1,5},{5,1},{2,6},{6,2},{3,7},{7,3},{8,12},{12,8},{9,1... | collective-permute-start | bytes 196616 | tf_op jit(solution)/shard_map/ppermute | solution.py:333
  23.6 23.6 %copy-start.8 = (bf16[256,128]{1,0:T(8,128)(2,1)}, bf16[256,128]{1,0:T(8,128)(2,1)S(1)}, u32[]{:S(2)}) copy-start(bf16[256,128]{1,0:T(8,128)(2,1)S(1)} %collective-permute-done.1) | copy-start | bytes 196612
  31.2 16.0 %all-to-all-start.3 = ((bf16[128,2,128]{2,1,0:T(2,128)(2,1)}), bf16[128,2,128]{2,1,0:T(2,128)(2,1)S(1)}, u32[]{:S(2)}, u32[]{:S(2)}) async-start(bf16[128,2,128]{2,1,0:T(2,128)(2,1)} %bitcast.8), calls=%async_computation.3 | async-start | bytes 131072 | tf_op jit(solution)/shard_map/all_to_all | solution.py:348
  49.3 60.3 %collective-permute-start.2 = (bf16[128,1024]{1,0:T(8,128)(2,1)}, bf16[128,1024]{1,0:T(8,128)(2,1)S(1)}, u32[]{:S(2)}, u32[]{:S(2)}) collective-permute-start(bf16[128,1024]{1,0:T(8,128)(2,1)} %get-tuple-element.67), channel_id=1, source_target_pairs={{0,2},{1,3},{2,0},{3,1},{4,6},{5,7},{6,4},{7,5},{8,10},{9,11},{10,... | collective-permute-start | bytes 786440 | tf_op jit(solution)/shard_map/ppermute | solution.py:333
  62.1 47.6 %collective-permute-start.3 = (bf16[128,1024]{1,0:T(8,128)(2,1)S(1)}, bf16[128,1024]{1,0:T(8,128)(2,1)}, u32[]{:S(2)}, u32[]{:S(2)}) collective-permute-start(bf16[128,1024]{1,0:T(8,128)(2,1)S(1)} %get-tuple-element.68), channel_id=1, source_target_pairs={{0,1},{1,2},{2,3},{3,0},{4,5},{5,6},{6,7},{7,4},{8,9},{9,10},{10,1... | collective-permute-start | bytes 786440 | tf_op jit(solution)/shard_map/ppermute | solution.py:333
  66.1 43.6 %collective-permute-start.4 = (bf16[128,1024]{1,0:T(8,128)(2,1)S(1)}, bf16[128,1024]{1,0:T(8,128)(2,1)}, u32[]{:S(2)}, u32[]{:S(2)}) collective-permute-start(bf16[128,1024]{1,0:T(8,128)(2,1)S(1)} %get-tuple-element.69), channel_id=1, source_target_pairs={{0,3},{1,0},{2,1},{3,2},{4,7},{5,4},{6,5},{7,6},{8,11},{9,8},{10,9... | collective-permute-start | bytes 786440 | tf_op jit(solution)/shard_map/ppermute | solution.py:333
  71.3 3.0 %copy-start.9 = (bf16[256,128]{1,0:T(8,128)(2,1)S(1)}, bf16[256,128]{1,0:T(8,128)(2,1)}, u32[]{:S(2)}) copy-start(bf16[256,128]{1,0:T(8,128)(2,1)} %copy-done.8) | copy-start | bytes 196612
  91.3 18.2 %all-to-all-start.1 = ((bf16[4,48,128]{2,1,0:T(8,128)(2,1)}), bf16[4,48,128]{2,1,0:T(8,128)(2,1)S(1)}, u32[]{:S(2)}, u32[]{:S(2)}) async-start(bf16[4,48,128]{2,1,0:T(8,128)(2,1)} %stage.1), calls=%async_computation.1 | async-start | bytes 98304 | tf_op jit(solution)/shard_map/while/body/all_to_all | solution.py:356
  109.6 1.9 %copy-start.10 = (bf16[3,32,64]{2,1,0:T(8,128)(2,1)}, bf16[3,32,64]{2,1,0:T(8,128)(2,1)S(1)}, u32[]{:S(2)}) copy-start(bf16[3,32,64]{2,1,0:T(8,128)(2,1)S(1)} %get-tuple-element.65) | copy-start | bytes 36868

commit v3 on v2

--- a/solution.py
+++ b/solution.py
@@ -252,6 +252,22 @@
     )(chan, got, fields, flat_w)
 
 
+def last_kernel(own_ref, *refs):
+    total = own_ref[...].astype(F32)
+    for ref in refs[:-1]:
+        total += ref[...].astype(F32)
+    refs[-1][...] = total.astype(BF16)
+
+
+def last_call(own, *others):
+    return pl.pallas_call(
+        last_kernel,
+        out_shape=jax.ShapeDtypeStruct(own.shape, BF16),
+        compiler_params=params(),
+        name="last",
+    )(own, *others)
+
+
 def share_kernel(before_ref, got_ref, own_ref, other_ref, flipped_ref, out_ref, scratch, grads):
     del before_ref
 
@@ -342,10 +358,12 @@
     other_inputs = turned(late_inputs, "core", 1)
     other_fields = turned(fields, "core", 1)
     got = lax.all_to_all(send.reshape(ROWS, 2, ROWS), SEQ, 0, 0, tiled=True)
-    got, other_inputs, other_fields = lax.optimization_barrier((got, other_inputs, other_fields))
+    got, other_fields = lax.optimization_barrier((got, other_fields))
+    conv = conv_call(got.reshape(2 * ROWS, ROWS))
+    conv, other_inputs = lax.optimization_barrier((conv, other_inputs))
     flipped = flip_call(inputs, other_inputs)
-    conv = conv_call(got.reshape(2 * ROWS, ROWS))
     got = lax.all_to_all(conv.reshape(ROWS, 2, ROWS), SEQ, 0, 0, tiled=True)
+    got, flipped = lax.optimization_barrier((got, flipped))
     got = got.reshape(2 * ROWS, ROWS)
     gated, grads, *parts = parts_call(chan, got, fields, flat_w)
     arrived = [turned(part, "chan", shift) for shift, part in zip((2, 1, 3), parts)]
@@ -360,10 +378,7 @@
     weight_grad = lax.fori_loop(0, once, weights, jnp.zeros((3, width // ROWS, CH), BF16))
     weight_grad, own = lax.optimization_barrier((weight_grad, parts[3]))
     weight_grad = jnp.transpose(weight_grad, (1, 0, 2))
-    total = own.astype(F32)
-    for part in arrived:
-        total = total + part.astype(F32)
-    input_grad = total.astype(BF16)
+    input_grad = last_call(own, *arrived)
     return (gated.T, weight_grad, input_grad)
 
 

time: 112 us -> 112 us (level)
  waiting for transfers between devices: 32.2 us -> 29.8 us
  local copies, waits for them, and re-layouts: 0.07 us -> 2.27 us
  other arithmetic: 1.9 us -> 0 us
  Pallas kernels: 11.8 us -> 13.7 us
    all_to_all x1, waiting for transfers between devices: 10.1 us -> 6.32 us  [shards(): got = lax.all_to_all(conv.reshape(ROWS, 2, ROWS), SEQ, 0, 0, tiled=True)]
    unnamed x22, local copies, waits for them, and re-layouts: 0.06 us -> 2.26 us
    convert_element_type x1 -> x0, other arithmetic: 1.9 us -> none  [shards(): input_grad = total.astype(BF16)]
    pallas_call x1, Pallas kernels: 1.34 us -> 2.96 us  [share_call(): pl.pallas_call(share_kernel, grid=(planes * steps // tile,), in_specs=[pl...]
    all_to_all x1, waiting for transfers between devices: 15 us -> 16.3 us  [weights(): share = lax.all_to_all(share, 'z', 0, 0, tiled=True)]
  transfers between devices with their start and end apart: 8 -> 8, of which waited for: 4 -> 4; matrix products, arithmetic and copies ran while one was open for 0% -> 0% of each run, Pallas kernels for 5% -> 7%
where the time goes in v3:
time: 112 us; the launch traced here: 111 us
  starting transfers between devices  49.8 us (44%)
  waiting for transfers between devices  29.8 us (27%)
  blocking collectives  14.7 us (13%)
  Pallas kernels  13.7 us (12%)
  local copies, waits for them, and re-layouts  2.27 us (2%)
    ppermute x5, starting transfers between devices, turned(): lax.ppermute(value, axis, [(i, (i + shift) % size) for i in range(size)])  33.5 us
    all_to_all x1, waiting for transfers between devices, weights(): share = lax.all_to_all(share, 'z', 0, 0, tiled=True)  16.3 us
    all_to_all x1, blocking collectives, weights(): share = stage_call(lax.all_to_all(share, ('x', 'y'), 0, 0, tiled=True))  14.7 us
    all_to_all x1, starting transfers between devices, shards(): got = lax.all_to_all(send.reshape(ROWS, 2, ROWS), SEQ, 0, 0, tiled=True)  7.09 us
    all_to_all x1, waiting for transfers between devices, shards(): got = lax.all_to_all(conv.reshape(ROWS, 2, ROWS), SEQ, 0, 0, tiled=True)  6.32 us
    all_to_all x1, waiting for transfers between devices, shards(): got = lax.all_to_all(send.reshape(ROWS, 2, ROWS), SEQ, 0, 0, tiled=True)  6.27 us
    all_to_all x1, starting transfers between devices, shards(): got = lax.all_to_all(conv.reshape(ROWS, 2, ROWS), SEQ, 0, 0, tiled=True)  5.89 us
    pallas_call x1, Pallas kernels, fields_call(): pl.pallas_call(fields_kernel, in_specs=[pl.BlockSpec(memory_space=pl.ANY)...  3.28 us
  transfers between devices with their start and end apart: 8, of which 4 were waited for; matrix products, arithmetic and copies ran while one was open for 0% of the time, Pallas kernels for 7%

profile of v3, /device:TPU:1, one launch (start us, length us, event | category | flops | bytes accessed | tf_op | source)
XLA Modules:
  0.0 111.0 jit_solution(5449248811571079543)
XLA Ops:
  0.6 0.0 copy-start.6
  0.6 0.0 copy-start.4
  0.7 0.0 copy-start.5
  0.7 0.0 copy-start.7
  0.7 0.0 copy-start.8
  0.7 0.0 copy-start.9
  0.7 3.3 %fields.1 = (bf16[256,128]{1,0:T(8,128)(2,1)S(1)}, bf16[256,128]{1,0:T(8,128)(2,1)}) custom-call(bf16[128,4096]{1,0:T(8,128)(2,1)} %x_ref.1, bf16[192,4096]{1,0:T(8,128)(2,1)} %bitcast.17, f32[64,128]{1,0:T(8,128)} %bitcast.25, bf16[64,128]{1,0:T(8,128)(2,1)} %bitcast.26), custom_call_target="tpu_custom_call" | custom-call | tf_op jit(solution)/shard_map/fields/pallas_call | solution.py:108
  4.0 8.8 %collective-permute-start.1 = (bf16[128,4096]{1,0:T(8,128)(2,1)S(1)}, bf16[128,4096]{1,0:T(8,128)(2,1)S(1)}, u32[]{:S(2)}, u32[]{:S(2)}) collective-permute-start(bf16[128,4096]{1,0:T(8,128)(2,1)S(1)} %copy-done.1), channel_id=1, source_target_pairs={{0,4},{4,0},{1,5},{5,1},{2,6},{6,2},{3,7},{7,3},{8,12},{12,8},{9,1... | collective-permute-start | bytes 3145736 | tf_op jit(solution)/shard_map/ppermute | solution.py:349
  12.8 7.1 %all-to-all-start.2 = ((bf16[128,2,128]{2,1,0:T(2,128)(2,1)}), bf16[128,2,128]{2,1,0:T(2,128)(2,1)S(1)}, u32[]{:S(2)}, u32[]{:S(2)}) async-start(bf16[128,2,128]{2,1,0:T(2,128)(2,1)} %bitcast.24), calls=%async_computation.2 | async-start | bytes 131072 | tf_op jit(solution)/shard_map/all_to_all | solution.py:360
  19.9 2.8 %collective-permute-start = (bf16[256,128]{1,0:T(8,128)(2,1)S(1)}, bf16[256,128]{1,0:T(8,128)(2,1)S(1)}, u32[]{:S(2)}, u32[]{:S(2)}) collective-permute-start(bf16[256,128]{1,0:T(8,128)(2,1)S(1)} %get-tuple-element.139.fields_ref), channel_id=1, source_target_pairs={{0,4},{4,0},{1,5},{5,1},{2,6},{6,2},{3,7},{7,3},{8,12},{12,8},{9,1... | collective-permute-start | bytes 196616 | tf_op jit(solution)/shard_map/ppermute | solution.py:349
  22.7 0.9 collective-permute-done
  23.6 6.3 %all-to-all-done.2 = bf16[128,2,128]{2,1,0:T(2,128)(2,1)S(1)} async-done(((bf16[128,2,128]{2,1,0:T(2,128)(2,1)}), bf16[128,2,128]{2,1,0:T(2,128)(2,1)S(1)}, u32[]{:S(2)}, u32[]{:S(2)}) %all-to-all-start.2) | async-done | bytes 65568 | tf_op jit(solution)/shard_map/all_to_all | solution.py:360
  29.9 1.3 %conv.1 = bf16[256,128]{1,0:T(8,128)(2,1)} custom-call(bf16[256,128]{1,0:T(8,128)(2,1)S(1)} %bitcast.19, bf16[256,128]{1,0:T(8,128)(2,1)S(1)} %copy-done.9, f32[128,128]{1,0:T(8,128)S(1)} %copy-done.8, f32[128,128]{1,0:T(8,128)S(1)} %copy-done.7, bf16[256,256]{1,0:T(8,128)(2,1)S(1)} %copy-done.5, bf16[256,256]{1,0:T(8,128)(2,1)S(1)} %copy-done.4, ...), custom_call_target="tpu_custom_call" | custom-call | tf_op jit(solution)/shard_map/conv/pallas_call | solution.py:184
  31.2 1.0 copy-done.2
  32.2 5.9 %all-to-all-start.3 = ((bf16[128,2,128]{2,1,0:T(2,128)(2,1)}), bf16[128,2,128]{2,1,0:T(2,128)(2,1)S(1)}, u32[]{:S(2)}, u32[]{:S(2)}) async-start(bf16[128,2,128]{2,1,0:T(2,128)(2,1)} %bitcast.8), calls=%async_computation.3 | async-start | bytes 131072 | tf_op jit(solution)/shard_map/all_to_all | solution.py:365
  38.1 1.2 %copy-done.3 = bf16[128,4096]{1,0:T(8,128)(2,1)S(1)} copy-done((bf16[128,4096]{1,0:T(8,128)(2,1)S(1)}, bf16[128,4096]{1,0:T(8,128)(2,1)}, u32[]{:S(2)}) %copy-start.3) | copy-done | bytes 1048600
  39.3 2.5 %flip.1 = bf16[16,4,32,256]{3,2,1,0:T(8,128)(2,1)} custom-call(bf16[128,4096]{1,0:T(8,128)(2,1)S(1)} %copy-done.1, bf16[128,4096]{1,0:T(8,128)(2,1)S(1)} %copy-done.3), custom_call_target="tpu_custom_call" | custom-call | tf_op jit(solution)/shard_map/flip/pallas_call | solution.py:138
  41.8 6.3 %all-to-all-done.3 = bf16[128,2,128]{2,1,0:T(2,128)(2,1)S(1)} async-done(((bf16[128,2,128]{2,1,0:T(2,128)(2,1)}), bf16[128,2,128]{2,1,0:T(2,128)(2,1)S(1)}, u32[]{:S(2)}, u32[]{:S(2)}) %all-to-all-start.3) | async-done | bytes 65568 | tf_op jit(solution)/shard_map/all_to_all | solution.py:365
  48.2 2.0 %parts.1 = (bf16[64,128]{1,0:T(8,128)(2,1)}, bf16[128,192]{1,0:T(8,128)(2,1)}, bf16[128,1024]{1,0:T(8,128)(2,1)S(1)}, bf16[128,1024]{1,0:T(8,128)(2,1)S(1)}, bf1...) custom-call(s32[1]{0:T(128)} %bitcast.2.chan_ref, bf16[256,128]{1,0:T(8,128)(2,1)S(1)} %bitcast.21, ...), custom_call_target="tpu_custom_call" | custom-call | tf_op jit(solution)/shard_map/parts/pallas_call | solution.py:230
  50.1 12.7 %collective-permute-start.2 = (bf16[128,1024]{1,0:T(8,128)(2,1)S(1)}, bf16[128,1024]{1,0:T(8,128)(2,1)S(1)}, u32[]{:S(2)}, u32[]{:S(2)}) collective-permute-start(bf16[128,1024]{1,0:T(8,128)(2,1)S(1)} %get-tuple-element.73), channel_id=1, source_target_pairs={{0,2},{1,3},{2,0},{3,1},{4,6},{5,7},{6,4},{7,5},{8,10},{9,11},{10,... | collective-permute-start | bytes 786440 | tf_op jit(solution)/shard_map/ppermute | solution.py:349
  62.9 4.0 %collective-permute-start.3 = (bf16[128,1024]{1,0:T(8,128)(2,1)S(1)}, bf16[128,1024]{1,0:T(8,128)(2,1)S(1)}, u32[]{:S(2)}, u32[]{:S(2)}) collective-permute-start(bf16[128,1024]{1,0:T(8,128)(2,1)S(1)} %get-tuple-element.74), channel_id=1, source_target_pairs={{0,1},{1,2},{2,3},{3,0},{4,5},{5,6},{6,7},{7,4},{8,9},{9,10},{10,1... | collective-permute-start | bytes 786440 | tf_op jit(solution)/shard_map/ppermute | solution.py:349
  66.9 5.2 %collective-permute-start.4 = (bf16[128,1024]{1,0:T(8,128)(2,1)S(1)}, bf16[128,1024]{1,0:T(8,128)(2,1)S(1)}, u32[]{:S(2)}, u32[]{:S(2)}) collective-permute-start(bf16[128,1024]{1,0:T(8,128)(2,1)S(1)} %get-tuple-element.75), channel_id=1, source_target_pairs={{0,3},{1,0},{2,1},{3,2},{4,7},{5,4},{6,5},{7,6},{8,11},{9,8},{10,9... | collective-permute-start | bytes 786440 | tf_op jit(solution)/shard_map/ppermute | solution.py:349
  72.1 38.1 %while.10 = (s32[]{:T(128)}, bf16[3,32,64]{2,1,0:T(8,128)(2,1)S(1)}, s32[]{:T(128)}, bf16[16,4,32,256]{3,2,1,0:T(8,128)(2,1)}, bf16[256,128]{1,0:T(8,128)(2,1)S(...) while((s32[]{:T(128)}, bf16[3,32,64]{2,1,0:T(8,128)(2,1)S(1)}, s32[]{:T(128)}, ...), condition=%wide.region_1.0_spmd, body=%wide.region_0.0_spmd.sunk | while | flops 2 | bytes 1720437 | solution.py:378
  72.1 3.0 %share.1 = bf16[64,48,128]{2,1,0:T(8,128)(2,1)S(1)} custom-call(bf16[3,32,64]{2,1,0:T(8,128)(2,1)S(1)} %get-tuple-element.143.before_ref, bf16[256,128]{1,0:T(8,128)(2,1)S(1)} %get-tuple-element.154.got_ref, bf16[256,128]{1,0:T(8,128)(2,1)S(1)} %get-tuple-element.155.own_ref, bf16[256,128]{1,0:T(8,128)(2,1)S(1)} %get-tuple-element.156.other_ref, ...), custom_call_target="tpu_custom_call" | custom-call | tf_op jit(solution)/shard_map/while/body/share/pallas_call | solution.py:294
  75.1 14.7 %all_to_all.22.got_ref = bf16[16,4,48,128]{3,2,1,0:T(8,128)(2,1)S(1)} all-to-all(bf16[16,4,48,128]{3,2,1,0:T(8,128)(2,1)S(1)} %bitcast.16), channel_id=1, replica_groups=mesh['z'=4,'x'=4,'y'=4,'core'=2,'chan'=4] {'x','y'}, dimensions={0} | all-to-all | bytes 1572864 | tf_op jit(solution)/shard_map/while/body/all_to_all | solution.py:373
  89.8 0.7 stage.1
  90.5 3.3 %all-to-all-start.1 = ((bf16[4,48,128]{2,1,0:T(8,128)(2,1)}), bf16[4,48,128]{2,1,0:T(8,128)(2,1)S(1)}, u32[]{:S(2)}, u32[]{:S(2)}) async-start(bf16[4,48,128]{2,1,0:T(8,128)(2,1)} %stage.1), calls=%async_computation.1 | async-start | bytes 98304 | tf_op jit(solution)/shard_map/while/body/all_to_all | solution.py:374
  93.8 16.3 %all-to-all-done.1.got_ref = bf16[4,48,128]{2,1,0:T(8,128)(2,1)S(1)} async-done(((bf16[4,48,128]{2,1,0:T(8,128)(2,1)}), bf16[4,48,128]{2,1,0:T(8,128)(2,1)S(1)}, u32[]{:S(2)}, u32[]{:S(2)}) %all-to-all-start.1) | async-done | bytes 49184 | tf_op jit(solution)/shard_map/while/body/all_to_all | solution.py:374
  110.1 0.1 total.1
  110.2 0.0 collective-permute-done.2.refs_0_
  110.2 0.0 collective-permute-done.3.refs_1_
  110.2 0.8 last.1
  (17 shorter events, 0.0 us)
Async XLA Ops:
  0.6 29.2 %copy-start.6 = (bf16[128,256]{1,0:T(8,128)(2,1)S(1)}, bf16[128,256]{1,0:T(8,128)(2,1)}, u32[]{:S(2)}) copy-start(bf16[128,256]{1,0:T(8,128)(2,1)} %constant.33.clone.e1b_ref) | copy-start | bytes 196612
  0.6 29.2 %copy-start.4 = (bf16[256,256]{1,0:T(8,128)(2,1)S(1)}, bf16[256,256]{1,0:T(8,128)(2,1)}, u32[]{:S(2)}) copy-start(bf16[256,256]{1,0:T(8,128)(2,1)} %constant.32.clone.e2b_ref) | copy-start | bytes 393220
  0.7 29.2 %copy-start.5 = (bf16[256,256]{1,0:T(8,128)(2,1)S(1)}, bf16[256,256]{1,0:T(8,128)(2,1)}, u32[]{:S(2)}) copy-start(bf16[256,256]{1,0:T(8,128)(2,1)} %constant.31.clone.e2_ref) | copy-start | bytes 393220
  0.7 29.2 %copy-start.7 = (f32[128,128]{1,0:T(8,128)S(1)}, f32[128,128]{1,0:T(8,128)}, u32[]{:S(2)}) copy-start(f32[128,128]{1,0:T(8,128)} %constant.30.clone.twi_ref) | copy-start | bytes 196612
  0.7 29.2 %copy-start.8 = (f32[128,128]{1,0:T(8,128)S(1)}, f32[128,128]{1,0:T(8,128)}, u32[]{:S(2)}) copy-start(f32[128,128]{1,0:T(8,128)} %constant.29.clone.twr_ref) | copy-start | bytes 196612
  0.7 29.2 %copy-start.9 = (bf16[256,128]{1,0:T(8,128)(2,1)S(1)}, bf16[256,128]{1,0:T(8,128)(2,1)}, u32[]{:S(2)}) copy-start(bf16[256,128]{1,0:T(8,128)(2,1)} %constant.28.clone.e1_ref) | copy-start | bytes 196612
  0.7 3.3 %copy-start.1 = (bf16[128,4096]{1,0:T(8,128)(2,1)S(1)}, bf16[128,4096]{1,0:T(8,128)(2,1)}, u32[]{:S(2)}) copy-start(bf16[128,4096]{1,0:T(8,128)(2,1)} %x_ref.1) | copy-start | bytes 3145732
  4.0 27.2 %collective-permute-start.1 = (bf16[128,4096]{1,0:T(8,128)(2,1)S(1)}, bf16[128,4096]{1,0:T(8,128)(2,1)S(1)}, u32[]{:S(2)}, u32[]{:S(2)}) collective-permute-start(bf16[128,4096]{1,0:T(8,128)(2,1)S(1)} %copy-done.1), channel_id=1, source_target_pairs={{0,4},{4,0},{1,5},{5,1},{2,6},{6,2},{3,7},{7,3},{8,12},{12,8},{9,1... | collective-permute-start | bytes 3145736 | tf_op jit(solution)/shard_map/ppermute | solution.py:349
  12.8 17.1 %all-to-all-start.2 = ((bf16[128,2,128]{2,1,0:T(2,128)(2,1)}), bf16[128,2,128]{2,1,0:T(2,128)(2,1)S(1)}, u32[]{:S(2)}, u32[]{:S(2)}) async-start(bf16[128,2,128]{2,1,0:T(2,128)(2,1)} %bitcast.24), calls=%async_computation.2 | async-start | bytes 131072 | tf_op jit(solution)/shard_map/all_to_all | solution.py:360
  19.9 3.7 %collective-permute-start = (bf16[256,128]{1,0:T(8,128)(2,1)S(1)}, bf16[256,128]{1,0:T(8,128)(2,1)S(1)}, u32[]{:S(2)}, u32[]{:S(2)}) collective-permute-start(bf16[256,128]{1,0:T(8,128)(2,1)S(1)} %get-tuple-element.139.fields_ref), channel_id=1, source_target_pairs={{0,4},{4,0},{1,5},{5,1},{2,6},{6,2},{3,7},{7,3},{8,12},{12,8},{9,1... | collective-permute-start | bytes 196616 | tf_op jit(solution)/shard_map/ppermute | solution.py:349
  31.2 1.0 copy-start.2
  32.2 16.0 %all-to-all-start.3 = ((bf16[128,2,128]{2,1,0:T(2,128)(2,1)}), bf16[128,2,128]{2,1,0:T(2,128)(2,1)S(1)}, u32[]{:S(2)}, u32[]{:S(2)}) async-start(bf16[128,2,128]{2,1,0:T(2,128)(2,1)} %bitcast.8), calls=%async_computation.3 | async-start | bytes 131072 | tf_op jit(solution)/shard_map/all_to_all | solution.py:365
  38.1 1.2 %copy-start.3 = (bf16[128,4096]{1,0:T(8,128)(2,1)S(1)}, bf16[128,4096]{1,0:T(8,128)(2,1)}, u32[]{:S(2)}) copy-start(bf16[128,4096]{1,0:T(8,128)(2,1)} %copy-done.2) | copy-start | bytes 3145732
  39.3 8.8 %copy-start = (bf16[3,64,4096]{2,1,0:T(8,128)(2,1)S(1)}, bf16[3,64,4096]{2,1,0:T(8,128)(2,1)}, u32[]{:S(2)}) copy-start(bf16[3,64,4096]{2,1,0:T(8,128)(2,1)} %param.13) | copy-start | bytes 4718596
  50.1 60.0 %collective-permute-start.2 = (bf16[128,1024]{1,0:T(8,128)(2,1)S(1)}, bf16[128,1024]{1,0:T(8,128)(2,1)S(1)}, u32[]{:S(2)}, u32[]{:S(2)}) collective-permute-start(bf16[128,1024]{1,0:T(8,128)(2,1)S(1)} %get-tuple-element.73), channel_id=1, source_target_pairs={{0,2},{1,3},{2,0},{3,1},{4,6},{5,7},{6,4},{7,5},{8,10},{9,11},{10,... | collective-permute-start | bytes 786440 | tf_op jit(solution)/shard_map/ppermute | solution.py:349
  62.9 47.3 %collective-permute-start.3 = (bf16[128,1024]{1,0:T(8,128)(2,1)S(1)}, bf16[128,1024]{1,0:T(8,128)(2,1)S(1)}, u32[]{:S(2)}, u32[]{:S(2)}) collective-permute-start(bf16[128,1024]{1,0:T(8,128)(2,1)S(1)} %get-tuple-element.74), channel_id=1, source_target_pairs={{0,1},{1,2},{2,3},{3,0},{4,5},{5,6},{6,7},{7,4},{8,9},{9,10},{10,1... | collective-permute-start | bytes 786440 | tf_op jit(solution)/shard_map/ppermute | solution.py:349
  66.9 43.3 %collective-permute-start.4 = (bf16[128,1024]{1,0:T(8,128)(2,1)S(1)}, bf16[128,1024]{1,0:T(8,128)(2,1)S(1)}, u32[]{:S(2)}, u32[]{:S(2)}) collective-permute-start(bf16[128,1024]{1,0:T(8,128)(2,1)S(1)} %get-tuple-element.75), channel_id=1, source_target_pairs={{0,3},{1,0},{2,1},{3,2},{4,7},{5,4},{6,5},{7,6},{8,11},{9,8},{10,9... | collective-permute-start | bytes 786440 | tf_op jit(solution)/shard_map/ppermute | solution.py:349
  90.5 19.6 %all-to-all-start.1 = ((bf16[4,48,128]{2,1,0:T(8,128)(2,1)}), bf16[4,48,128]{2,1,0:T(8,128)(2,1)S(1)}, u32[]{:S(2)}, u32[]{:S(2)}) async-start(bf16[4,48,128]{2,1,0:T(8,128)(2,1)} %stage.1), calls=%async_computation.1 | async-start | bytes 98304 | tf_op jit(solution)/shard_map/while/body/all_to_all | solution.py:374
  110.2 0.9 copy-start.10

commit v4 on v3

--- a/solution.py
+++ b/solution.py
@@ -358,12 +358,10 @@
     other_inputs = turned(late_inputs, "core", 1)
     other_fields = turned(fields, "core", 1)
     got = lax.all_to_all(send.reshape(ROWS, 2, ROWS), SEQ, 0, 0, tiled=True)
-    got, other_fields = lax.optimization_barrier((got, other_fields))
+    got, other_inputs, other_fields = lax.optimization_barrier((got, other_inputs, other_fields))
+    flipped = flip_call(inputs, other_inputs)
     conv = conv_call(got.reshape(2 * ROWS, ROWS))
-    conv, other_inputs = lax.optimization_barrier((conv, other_inputs))
-    flipped = flip_call(inputs, other_inputs)
     got = lax.all_to_all(conv.reshape(ROWS, 2, ROWS), SEQ, 0, 0, tiled=True)
-    got, flipped = lax.optimization_barrier((got, flipped))
     got = got.reshape(2 * ROWS, ROWS)
     gated, grads, *parts = parts_call(chan, got, fields, flat_w)
     arrived = [turned(part, "chan", shift) for shift, part in zip((2, 1, 3), parts)]

time: 112 us -> 111 us (level)
  local copies, waits for them, and re-layouts: 2.27 us -> 0.07 us
  Pallas kernels: 13.7 us -> 15.3 us
    all_to_all x1, waiting for transfers between devices: 16.3 us -> 12.5 us  [weights(): share = lax.all_to_all(share, 'z', 0, 0, tiled=True)]
    all_to_all x1, waiting for transfers between devices: 6.32 us -> 10.1 us  [shards(): got = lax.all_to_all(conv.reshape(ROWS, 2, ROWS), SEQ, 0, 0, tiled=True)]
    unnamed x22, local copies, waits for them, and re-layouts: 2.26 us -> 0.06 us
    pallas_call x1, Pallas kernels: 2.52 us -> 4.02 us  [flip_call(): pl.pallas_call(flip_kernel, grid=(steps,), in_specs=[pl.BlockSpec((ROWS,...]
where the time goes in v4:
time: 111 us; the launch traced here: 110 us
  starting transfers between devices  49.8 us (45%)
  waiting for transfers between devices  29.7 us (27%)
  Pallas kernels  15.3 us (14%)
  blocking collectives  14.7 us (13%)
    ppermute x5, starting transfers between devices, turned(): lax.ppermute(value, axis, [(i, (i + shift) % size) for i in range(size)])  33.5 us
    all_to_all x1, blocking collectives, weights(): share = stage_call(lax.all_to_all(share, ('x', 'y'), 0, 0, tiled=True))  14.7 us
    all_to_all x1, waiting for transfers between devices, weights(): share = lax.all_to_all(share, 'z', 0, 0, tiled=True)  12.5 us
    all_to_all x1, waiting for transfers between devices, shards(): got = lax.all_to_all(conv.reshape(ROWS, 2, ROWS), SEQ, 0, 0, tiled=True)  10.1 us
    all_to_all x1, starting transfers between devices, shards(): got = lax.all_to_all(send.reshape(ROWS, 2, ROWS), SEQ, 0, 0, tiled=True)  7.08 us
    all_to_all x1, waiting for transfers between devices, shards(): got = lax.all_to_all(send.reshape(ROWS, 2, ROWS), SEQ, 0, 0, tiled=True)  6.27 us
    all_to_all x1, starting transfers between devices, shards(): got = lax.all_to_all(conv.reshape(ROWS, 2, ROWS), SEQ, 0, 0, tiled=True)  5.89 us
    pallas_call x1, Pallas kernels, flip_call(): pl.pallas_call(flip_kernel, grid=(steps,), in_specs=[pl.BlockSpec((ROWS,...  4.02 us
  transfers between devices with their start and end apart: 8, of which 4 were waited for; matrix products, arithmetic and copies ran while one was open for 0% of the time, Pallas kernels for 7%

profile of v4, /device:TPU:1, one launch (start us, length us, event | category | flops | bytes accessed | tf_op | source)
XLA Modules:
  0.0 110.5 jit_solution(1879768067673870944)
XLA Ops:
  0.6 0.0 copy-start.4
  0.6 0.0 copy-start.2
  0.7 0.0 copy-start.3
  0.7 0.0 copy-start.5
  0.7 0.0 copy-start.6
  0.7 0.0 copy-start.7
  0.7 3.3 %fields.1 = (bf16[256,128]{1,0:T(8,128)(2,1)S(1)}, bf16[256,128]{1,0:T(8,128)(2,1)}) custom-call(bf16[128,4096]{1,0:T(8,128)(2,1)} %x_ref.1, bf16[192,4096]{1,0:T(8,128)(2,1)} %bitcast.17, f32[64,128]{1,0:T(8,128)} %bitcast.25, bf16[64,128]{1,0:T(8,128)(2,1)} %bitcast.26), custom_call_target="tpu_custom_call" | custom-call | tf_op jit(solution)/shard_map/fields/pallas_call | solution.py:108
  4.1 8.8 %collective-permute-start = (bf16[128,4096]{1,0:T(8,128)(2,1)S(1)}, bf16[128,4096]{1,0:T(8,128)(2,1)}, u32[]{:S(2)}, u32[]{:S(2)}) collective-permute-start(bf16[128,4096]{1,0:T(8,128)(2,1)S(1)} %copy-done.1), channel_id=1, source_target_pairs={{0,4},{4,0},{1,5},{5,1},{2,6},{6,2},{3,7},{7,3},{8,12},{12,8},{9,1... | collective-permute-start | bytes 3145736 | tf_op jit(solution)/shard_map/ppermute | solution.py:349
  12.9 7.1 %all-to-all-start.2 = ((bf16[128,2,128]{2,1,0:T(2,128)(2,1)}), bf16[128,2,128]{2,1,0:T(2,128)(2,1)S(1)}, u32[]{:S(2)}, u32[]{:S(2)}) async-start(bf16[128,2,128]{2,1,0:T(2,128)(2,1)} %bitcast.24), calls=%async_computation.2 | async-start | bytes 131072 | tf_op jit(solution)/shard_map/all_to_all | solution.py:360
  19.9 2.8 %collective-permute-start.1 = (bf16[256,128]{1,0:T(8,128)(2,1)S(1)}, bf16[256,128]{1,0:T(8,128)(2,1)S(1)}, u32[]{:S(2)}, u32[]{:S(2)}) collective-permute-start(bf16[256,128]{1,0:T(8,128)(2,1)S(1)} %get-tuple-element.133.fields_ref), channel_id=1, source_target_pairs={{0,4},{4,0},{1,5},{5,1},{2,6},{6,2},{3,7},{7,3},{8,12},{12,8},{9,1... | collective-permute-start | bytes 196616 | tf_op jit(solution)/shard_map/ppermute | solution.py:349
  22.8 0.9 collective-permute-done.1
  23.6 6.3 %all-to-all-done.2 = bf16[128,2,128]{2,1,0:T(2,128)(2,1)S(1)} async-done(((bf16[128,2,128]{2,1,0:T(2,128)(2,1)}), bf16[128,2,128]{2,1,0:T(2,128)(2,1)S(1)}, u32[]{:S(2)}, u32[]{:S(2)}) %all-to-all-start.2) | async-done | bytes 65568 | tf_op jit(solution)/shard_map/all_to_all | solution.py:360
  29.9 0.0 collective-permute-done.other_ref
  30.0 1.3 %conv.1 = bf16[256,128]{1,0:T(8,128)(2,1)} custom-call(bf16[256,128]{1,0:T(8,128)(2,1)S(1)} %bitcast.19, bf16[256,128]{1,0:T(8,128)(2,1)S(1)} %copy-done.7, f32[128,128]{1,0:T(8,128)S(1)} %copy-done.6, f32[128,128]{1,0:T(8,128)S(1)} %copy-done.5, bf16[256,256]{1,0:T(8,128)(2,1)S(1)} %copy-done.3, bf16[256,256]{1,0:T(8,128)(2,1)S(1)} %copy-done.2, ...), custom_call_target="tpu_custom_call" | custom-call | tf_op jit(solution)/shard_map/conv/pallas_call | solution.py:184
  31.2 5.9 %all-to-all-start.3 = ((bf16[128,2,128]{2,1,0:T(2,128)(2,1)}), bf16[128,2,128]{2,1,0:T(2,128)(2,1)S(1)}, u32[]{:S(2)}, u32[]{:S(2)}) async-start(bf16[128,2,128]{2,1,0:T(2,128)(2,1)} %bitcast.8), calls=%async_computation.3 | async-start | bytes 131072 | tf_op jit(solution)/shard_map/all_to_all | solution.py:364
  37.1 10.1 %all-to-all-done.3 = bf16[128,2,128]{2,1,0:T(2,128)(2,1)S(1)} async-done(((bf16[128,2,128]{2,1,0:T(2,128)(2,1)}), bf16[128,2,128]{2,1,0:T(2,128)(2,1)S(1)}, u32[]{:S(2)}, u32[]{:S(2)}) %all-to-all-start.3) | async-done | bytes 65568 | tf_op jit(solution)/shard_map/all_to_all | solution.py:364
  47.2 2.1 %parts.1 = (bf16[64,128]{1,0:T(8,128)(2,1)}, bf16[128,192]{1,0:T(8,128)(2,1)}, bf16[128,1024]{1,0:T(8,128)(2,1)}, bf16[128,1024]{1,0:T(8,128)(2,1)S(1)}, bf16[12...) custom-call(s32[1]{0:T(128)} %bitcast.2.chan_ref, bf16[256,128]{1,0:T(8,128)(2,1)S(1)} %bitcast.21, ...), custom_call_target="tpu_custom_call" | custom-call | tf_op jit(solution)/shard_map/parts/pallas_call | solution.py:230
  49.3 12.7 %collective-permute-start.2 = (bf16[128,1024]{1,0:T(8,128)(2,1)}, bf16[128,1024]{1,0:T(8,128)(2,1)S(1)}, u32[]{:S(2)}, u32[]{:S(2)}) collective-permute-start(bf16[128,1024]{1,0:T(8,128)(2,1)} %get-tuple-element.67), channel_id=1, source_target_pairs={{0,2},{1,3},{2,0},{3,1},{4,6},{5,7},{6,4},{7,5},{8,10},{9,11},{10,... | collective-permute-start | bytes 786440 | tf_op jit(solution)/shard_map/ppermute | solution.py:349
  62.1 4.0 %collective-permute-start.3 = (bf16[128,1024]{1,0:T(8,128)(2,1)S(1)}, bf16[128,1024]{1,0:T(8,128)(2,1)S(1)}, u32[]{:S(2)}, u32[]{:S(2)}) collective-permute-start(bf16[128,1024]{1,0:T(8,128)(2,1)S(1)} %get-tuple-element.68), channel_id=1, source_target_pairs={{0,1},{1,2},{2,3},{3,0},{4,5},{5,6},{6,7},{7,4},{8,9},{9,10},{10,1... | collective-permute-start | bytes 786440 | tf_op jit(solution)/shard_map/ppermute | solution.py:349
  66.1 5.2 %collective-permute-start.4 = (bf16[128,1024]{1,0:T(8,128)(2,1)S(1)}, bf16[128,1024]{1,0:T(8,128)(2,1)S(1)}, u32[]{:S(2)}, u32[]{:S(2)}) collective-permute-start(bf16[128,1024]{1,0:T(8,128)(2,1)S(1)} %get-tuple-element.69), channel_id=1, source_target_pairs={{0,3},{1,0},{2,1},{3,2},{4,7},{5,4},{6,5},{7,6},{8,11},{9,8},{10,9... | collective-permute-start | bytes 786440 | tf_op jit(solution)/shard_map/ppermute | solution.py:349
  71.3 4.0 %flip.1 = bf16[16,4,32,256]{3,2,1,0:T(8,128)(2,1)} custom-call(bf16[128,4096]{1,0:T(8,128)(2,1)S(1)} %copy-done.1, bf16[128,4096]{1,0:T(8,128)(2,1)} %collective-permute-done.other_ref), custom_call_target="tpu_custom_call" | custom-call | tf_op jit(solution)/shard_map/flip/pallas_call | solution.py:138
  75.3 34.3 %while.10 = (s32[]{:T(128)}, bf16[3,32,64]{2,1,0:T(8,128)(2,1)S(1)}, s32[]{:T(128)}, bf16[16,4,32,256]{3,2,1,0:T(8,128)(2,1)}, bf16[256,128]{1,0:T(8,128)(2,1)S(...) while((s32[]{:T(128)}, bf16[3,32,64]{2,1,0:T(8,128)(2,1)S(1)}, s32[]{:T(128)}, ...), condition=%wide.region_1.0_spmd, body=%wide.region_0.0_spmd.sunk | while | flops 2 | bytes 1720437 | solution.py:376
  75.3 3.0 %share.1 = bf16[64,48,128]{2,1,0:T(8,128)(2,1)S(1)} custom-call(bf16[3,32,64]{2,1,0:T(8,128)(2,1)S(1)} %get-tuple-element.137.before_ref, bf16[256,128]{1,0:T(8,128)(2,1)S(1)} %get-tuple-element.148.got_ref, bf16[256,128]{1,0:T(8,128)(2,1)S(1)} %get-tuple-element.149.own_ref, bf16[256,128]{1,0:T(8,128)(2,1)S(1)} %get-tuple-element.150.other_ref, ...), custom_call_target="tpu_custom_call" | custom-call | tf_op jit(solution)/shard_map/while/body/share/pallas_call | solution.py:294
  78.3 14.7 %all_to_all.22.got_ref = bf16[16,4,48,128]{3,2,1,0:T(8,128)(2,1)S(1)} all-to-all(bf16[16,4,48,128]{3,2,1,0:T(8,128)(2,1)S(1)} %bitcast.16), channel_id=1, replica_groups=mesh['z'=4,'x'=4,'y'=4,'core'=2,'chan'=4] {'x','y'}, dimensions={0} | all-to-all | bytes 1572864 | tf_op jit(solution)/shard_map/while/body/all_to_all | solution.py:371
  93.0 0.7 stage.1
  93.8 3.3 %all-to-all-start.1 = ((bf16[4,48,128]{2,1,0:T(8,128)(2,1)}), bf16[4,48,128]{2,1,0:T(8,128)(2,1)S(1)}, u32[]{:S(2)}, u32[]{:S(2)}) async-start(bf16[4,48,128]{2,1,0:T(8,128)(2,1)} %stage.1), calls=%async_computation.1 | async-start | bytes 98304 | tf_op jit(solution)/shard_map/while/body/all_to_all | solution.py:372
  97.0 12.5 %all-to-all-done.1.got_ref = bf16[4,48,128]{2,1,0:T(8,128)(2,1)S(1)} async-done(((bf16[4,48,128]{2,1,0:T(8,128)(2,1)}), bf16[4,48,128]{2,1,0:T(8,128)(2,1)S(1)}, u32[]{:S(2)}, u32[]{:S(2)}) %all-to-all-start.1) | async-done | bytes 49184 | tf_op jit(solution)/shard_map/while/body/all_to_all | solution.py:372
  109.5 0.1 total.1
  109.6 0.0 collective-permute-done.2.refs_0_
  109.6 0.0 collective-permute-done.3.refs_1_
  109.6 0.0 collective-permute-done.4.refs_2_
  109.6 0.8 last.1
  (17 shorter events, 0.0 us)
Async XLA Ops:
  0.6 29.3 %copy-start.4 = (bf16[128,256]{1,0:T(8,128)(2,1)S(1)}, bf16[128,256]{1,0:T(8,128)(2,1)}, u32[]{:S(2)}) copy-start(bf16[128,256]{1,0:T(8,128)(2,1)} %constant.33.clone.e1b_ref) | copy-start | bytes 196612
  0.6 29.3 %copy-start.2 = (bf16[256,256]{1,0:T(8,128)(2,1)S(1)}, bf16[256,256]{1,0:T(8,128)(2,1)}, u32[]{:S(2)}) copy-start(bf16[256,256]{1,0:T(8,128)(2,1)} %constant.32.clone.e2b_ref) | copy-start | bytes 393220
  0.7 29.3 %copy-start.3 = (bf16[256,256]{1,0:T(8,128)(2,1)S(1)}, bf16[256,256]{1,0:T(8,128)(2,1)}, u32[]{:S(2)}) copy-start(bf16[256,256]{1,0:T(8,128)(2,1)} %constant.31.clone.e2_ref) | copy-start | bytes 393220
  0.7 29.3 %copy-start.5 = (f32[128,128]{1,0:T(8,128)S(1)}, f32[128,128]{1,0:T(8,128)}, u32[]{:S(2)}) copy-start(f32[128,128]{1,0:T(8,128)} %constant.30.clone.twi_ref) | copy-start | bytes 196612
  0.7 29.3 %copy-start.6 = (f32[128,128]{1,0:T(8,128)S(1)}, f32[128,128]{1,0:T(8,128)}, u32[]{:S(2)}) copy-start(f32[128,128]{1,0:T(8,128)} %constant.29.clone.twr_ref) | copy-start | bytes 196612
  0.7 29.3 %copy-start.7 = (bf16[256,128]{1,0:T(8,128)(2,1)S(1)}, bf16[256,128]{1,0:T(8,128)(2,1)}, u32[]{:S(2)}) copy-start(bf16[256,128]{1,0:T(8,128)(2,1)} %constant.28.clone.e1_ref) | copy-start | bytes 196612
  0.7 3.3 %copy-start.1 = (bf16[128,4096]{1,0:T(8,128)(2,1)S(1)}, bf16[128,4096]{1,0:T(8,128)(2,1)}, u32[]{:S(2)}) copy-start(bf16[128,4096]{1,0:T(8,128)(2,1)} %x_ref.1) | copy-start | bytes 3145732
  0.7 46.5 %copy-start = (bf16[3,64,4096]{2,1,0:T(8,128)(2,1)S(1)}, bf16[3,64,4096]{2,1,0:T(8,128)(2,1)}, u32[]{:S(2)}) copy-start(bf16[3,64,4096]{2,1,0:T(8,128)(2,1)} %param.13) | copy-start | bytes 4718596
  4.1 25.9 %collective-permute-start = (bf16[128,4096]{1,0:T(8,128)(2,1)S(1)}, bf16[128,4096]{1,0:T(8,128)(2,1)}, u32[]{:S(2)}, u32[]{:S(2)}) collective-permute-start(bf16[128,4096]{1,0:T(8,128)(2,1)S(1)} %copy-done.1), channel_id=1, source_target_pairs={{0,4},{4,0},{1,5},{5,1},{2,6},{6,2},{3,7},{7,3},{8,12},{12,8},{9,1... | collective-permute-start | bytes 3145736 | tf_op jit(solution)/shard_map/ppermute | solution.py:349
  12.9 17.1 %all-to-all-start.2 = ((bf16[128,2,128]{2,1,0:T(2,128)(2,1)}), bf16[128,2,128]{2,1,0:T(2,128)(2,1)S(1)}, u32[]{:S(2)}, u32[]{:S(2)}) async-start(bf16[128,2,128]{2,1,0:T(2,128)(2,1)} %bitcast.24), calls=%async_computation.2 | async-start | bytes 131072 | tf_op jit(solution)/shard_map/all_to_all | solution.py:360
  19.9 3.7 %collective-permute-start.1 = (bf16[256,128]{1,0:T(8,128)(2,1)S(1)}, bf16[256,128]{1,0:T(8,128)(2,1)S(1)}, u32[]{:S(2)}, u32[]{:S(2)}) collective-permute-start(bf16[256,128]{1,0:T(8,128)(2,1)S(1)} %get-tuple-element.133.fields_ref), channel_id=1, source_target_pairs={{0,4},{4,0},{1,5},{5,1},{2,6},{6,2},{3,7},{7,3},{8,12},{12,8},{9,1... | collective-permute-start | bytes 196616 | tf_op jit(solution)/shard_map/ppermute | solution.py:349
  23.6 23.6 %copy-start.8 = (bf16[256,128]{1,0:T(8,128)(2,1)}, bf16[256,128]{1,0:T(8,128)(2,1)S(1)}, u32[]{:S(2)}) copy-start(bf16[256,128]{1,0:T(8,128)(2,1)S(1)} %collective-permute-done.1) | copy-start | bytes 196612
  31.2 16.0 %all-to-all-start.3 = ((bf16[128,2,128]{2,1,0:T(2,128)(2,1)}), bf16[128,2,128]{2,1,0:T(2,128)(2,1)S(1)}, u32[]{:S(2)}, u32[]{:S(2)}) async-start(bf16[128,2,128]{2,1,0:T(2,128)(2,1)} %bitcast.8), calls=%async_computation.3 | async-start | bytes 131072 | tf_op jit(solution)/shard_map/all_to_all | solution.py:364
  49.3 60.3 %collective-permute-start.2 = (bf16[128,1024]{1,0:T(8,128)(2,1)}, bf16[128,1024]{1,0:T(8,128)(2,1)S(1)}, u32[]{:S(2)}, u32[]{:S(2)}) collective-permute-start(bf16[128,1024]{1,0:T(8,128)(2,1)} %get-tuple-element.67), channel_id=1, source_target_pairs={{0,2},{1,3},{2,0},{3,1},{4,6},{5,7},{6,4},{7,5},{8,10},{9,11},{10,... | collective-permute-start | bytes 786440 | tf_op jit(solution)/shard_map/ppermute | solution.py:349
  62.1 47.6 %collective-permute-start.3 = (bf16[128,1024]{1,0:T(8,128)(2,1)S(1)}, bf16[128,1024]{1,0:T(8,128)(2,1)S(1)}, u32[]{:S(2)}, u32[]{:S(2)}) collective-permute-start(bf16[128,1024]{1,0:T(8,128)(2,1)S(1)} %get-tuple-element.68), channel_id=1, source_target_pairs={{0,1},{1,2},{2,3},{3,0},{4,5},{5,6},{6,7},{7,4},{8,9},{9,10},{10,1... | collective-permute-start | bytes 786440 | tf_op jit(solution)/shard_map/ppermute | solution.py:349
  66.1 43.6 %collective-permute-start.4 = (bf16[128,1024]{1,0:T(8,128)(2,1)S(1)}, bf16[128,1024]{1,0:T(8,128)(2,1)S(1)}, u32[]{:S(2)}, u32[]{:S(2)}) collective-permute-start(bf16[128,1024]{1,0:T(8,128)(2,1)S(1)} %get-tuple-element.69), channel_id=1, source_target_pairs={{0,3},{1,0},{2,1},{3,2},{4,7},{5,4},{6,5},{7,6},{8,11},{9,8},{10,9... | collective-permute-start | bytes 786440 | tf_op jit(solution)/shard_map/ppermute | solution.py:349
  71.3 4.0 %copy-start.9 = (bf16[256,128]{1,0:T(8,128)(2,1)S(1)}, bf16[256,128]{1,0:T(8,128)(2,1)}, u32[]{:S(2)}) copy-start(bf16[256,128]{1,0:T(8,128)(2,1)} %copy-done.8) | copy-start | bytes 196612
  93.8 15.8 %all-to-all-start.1 = ((bf16[4,48,128]{2,1,0:T(8,128)(2,1)}), bf16[4,48,128]{2,1,0:T(8,128)(2,1)S(1)}, u32[]{:S(2)}, u32[]{:S(2)}) async-start(bf16[4,48,128]{2,1,0:T(8,128)(2,1)} %stage.1), calls=%async_computation.1 | async-start | bytes 98304 | tf_op jit(solution)/shard_map/while/body/all_to_all | solution.py:372
  109.6 0.9 copy-start.10
